TPU v7x, 128 devices: a whole 4x4x4 slice. The times are simulated.
128 devices in a mesh: section: 16 (over x, z), head: 8 (over y, core).
Axes of the slice: x: 4, y: 4, z: 4, core: 2. Of those that a mesh axis runs over, the one named last changes fastest.
Arguments:
- kv_cache: bfloat16 [2, 32, 2048, 576], P(None, 'section', 'head'), may hold values from -6 to 6
- prompt_len: int32 [32], replicated, may hold values from 1 to 2048, 32768 in all
- assign: int32 [32], replicated, may hold values from 0 to 31, each once
- row_slot: int32 [512], P('section'), may hold values from 0 to 1
- q_nope: bfloat16 [2, 2, 512, 16384], P(None, None, 'section', 'head'), may hold values from -6 to 6
- q_rope: bfloat16 [2, 2, 512, 8192], P(None, None, 'section', 'head'), may hold values from -500 to 500
- new_kv: bfloat16 [2, 2, 512, 576], P(None, None, 'section'), may hold values from -6 to 6
- w_uk: bfloat16 [2, 128, 128, 512], P(None, 'head'), may hold values from -0.5 to 0.5
- w_uv: bfloat16 [2, 128, 512, 128], P(None, 'head'), may hold values from -0.25 to 0.25
Outputs:
- head_out: bfloat16 [2, 2, 512, 16384], P(None, None, 'section', 'head')
All inputs are finite; a program needn't handle non-finite values.
Results may differ from a plain program's by a relative error of at most 0.012.
Values may be sent and summed in bfloat16 or wider, within the bound.
No kernel may reach another device: no remote copies, remote signals or barrier semaphores. Data moves between devices by JAX's collectives and lax.ppermute only.
A program may use at most 128 MiB of HBM per device.

v0:
```python
import functools
import math

import jax
import jax.numpy as jnp
from jax import lax
from jax.experimental import pallas as pl
from jax.experimental.pallas import tpu as pltpu
from jax.sharding import PartitionSpec as P

BF = jnp.bfloat16
F32 = jnp.float32
TILE_ROWS = 8
LOW = -1e30
MIB = 1 << 20


def params(limit, **extra):
    return pltpu.CompilerParams(vmem_limit_bytes=limit * MIB, **extra)


def cost(flops, nbytes, trans=0):
    return pl.CostEstimate(flops=int(flops), bytes_accessed=int(nbytes), transcendentals=int(trans))


def pack_body(lat, kv_ref, x0_ref, x1_ref):
    parts = x0_ref.shape[0]
    rows = x0_ref.shape[2]
    a = kv_ref[0, 0]
    b = kv_ref[1, 0]
    x0 = jnp.concatenate([a[:, :lat], a[:, lat:], b[:, lat:]], axis=1)
    x0_ref[:, 0] = x0.reshape(parts, rows, x0.shape[1])
    x1_ref[:, 0] = b[:, :lat].reshape(parts, rows, lat)


def pack(kv, parts, lat):
    layers, prompts, tok, width = kv.shape
    wide = lat + 2 * (width - lat)
    rows = tok // parts
    return pl.pallas_call(
        functools.partial(pack_body, lat),
        grid=(prompts,),
        in_specs=[pl.BlockSpec((layers, 1, tok, width), lambda p: (0, p, 0, 0))],
        out_specs=[
            pl.BlockSpec((parts, 1, rows, wide), lambda p: (0, p, 0, 0)),
            pl.BlockSpec((parts, 1, rows, lat), lambda p: (0, p, 0, 0)),
        ],
        out_shape=[
            jax.ShapeDtypeStruct((parts, prompts, rows, wide), BF),
            jax.ShapeDtypeStruct((parts, prompts, rows, lat), BF),
        ],
        compiler_params=params(16),
        cost_estimate=cost(0, 2 * kv.size * 2),
        name="pack",
    )(kv)


def pick_body(assign_ref, x_ref, o_ref):
    for i in range(o_ref.shape[0]):
        o_ref[i] = x_ref[assign_ref[i]]


def pick(assign, x):
    flat = x.reshape((-1,) + x.shape[2:])
    out = pl.pallas_call(
        pick_body,
        in_specs=[
            pl.BlockSpec(memory_space=pltpu.SMEM),
            pl.BlockSpec(memory_space=pltpu.VMEM),
        ],
        out_specs=pl.BlockSpec(memory_space=pltpu.VMEM),
        out_shape=jax.ShapeDtypeStruct(flat.shape, BF),
        compiler_params=params(16),
        cost_estimate=cost(0, 2 * x.size * 2),
        name="pick",
    )(assign, flat)
    return out.reshape(x.shape)


def row_places(slot_ref):
    n = slot_ref.shape[0]
    ones = jnp.int32(0)
    for r in range(n):
        ones = ones + slot_ref[r]
    zeros = n - ones
    tiles0 = lax.div(zeros + (TILE_ROWS - 1), jnp.int32(TILE_ROWS))
    tiles1 = lax.div(ones + (TILE_ROWS - 1), jnp.int32(TILE_ROWS))
    places = []
    c0, c1 = jnp.int32(0), tiles0 * TILE_ROWS
    for r in range(n):
        s = slot_ref[r]
        places.append(jnp.where(s == 0, c0, c1))
        c0 = c0 + (1 - s)
        c1 = c1 + s
    return places, tiles0, tiles1


def order_index(axis, shape, steps):
    i = lax.broadcasted_iota(jnp.int32, shape, axis)
    per = TILE_ROWS * steps
    tile = i // per
    rest = i - tile * per
    step = rest // TILE_ROWS
    return tile * TILE_ROWS + (rest - step * TILE_ROWS), step


def split3(x):
    hi = x.astype(BF).astype(F32)
    mid = (x - hi).astype(BF).astype(F32)
    lo = x - hi - mid
    return hi, mid, lo


def with_lse(o, lse):
    hi, mid, lo = split3(lse)
    lane = lax.broadcasted_iota(jnp.int32, (o.shape[0], 128), 1)
    tail = jnp.where(lane == 0, hi, jnp.where(lane == 1, mid, jnp.where(lane == 2, lo, 0.0)))
    return jnp.concatenate([o.astype(BF), tail.astype(BF)], axis=1)


def query_body(layer, steps, scale, slot_ref, nope_ref, rope_ref, w_ref, nk_ref, q_ref, n_ref, perm_ref, own_ref):
    tiles, heads, per, wide = q_ref.shape
    rows = nope_ref.shape[2]
    nope = w_ref.shape[2]
    lat = w_ref.shape[3]
    total = tiles * per

    @pl.when(pl.program_id(0) == 0)
    def _():
        places, _, _ = row_places(slot_ref)
        lane = lax.broadcasted_iota(jnp.int32, (1, steps * rows), 1)
        step_of = lane // rows
        row_of = lane - step_of * rows
        where_to = jnp.full((1, steps * rows), -1, jnp.int32)
        for r in range(rows):
            where_to = jnp.where(row_of == r, places[r], where_to)
        place, step = order_index(0, (total, steps * rows), steps)
        perm_ref[...] = jnp.where((place == where_to) & (step == step_of), 1.0, 0.0).astype(BF)
        lane1 = lax.broadcasted_iota(jnp.int32, (total, rows), 1)
        place1, _ = order_index(0, (total, rows), steps)
        where1 = jnp.full((1, rows), -1, jnp.int32)
        lane_r = lax.broadcasted_iota(jnp.int32, (1, rows), 1)
        for r in range(rows):
            where1 = jnp.where(lane_r == r, places[r], where1)
        by_row = jnp.where(place1 == where1, 1.0, 0.0).astype(BF)
        for s in range(steps):
            own_ref[s] = jnp.dot(by_row, nk_ref[s, 0], preferred_element_type=F32)

    perm = perm_ref[...]
    x = nope_ref[:, 0].reshape(steps * rows, heads * nope)
    x = jnp.dot(perm, x, preferred_element_type=F32).astype(BF)
    r = rope_ref[:, 0].reshape(steps * rows, 128)
    r = jnp.dot(perm, r, preferred_element_type=F32)
    rolled = pltpu.roll(r, 64, 1)
    lane = lax.broadcasted_iota(jnp.int32, (total, 128), 1)
    mine = (lane // 64) == layer
    _, step = order_index(0, (total, 1), steps)
    for h in range(heads):
        ql = jnp.dot(x[:, h * nope:(h + 1) * nope], w_ref[0, h], preferred_element_type=F32).astype(BF)
        qr = jnp.where(mine, r if h == layer else rolled, 0.0).astype(BF)
        q = jnp.concatenate([ql, qr], axis=1)
        q_ref[:, h] = q.reshape(tiles, per, wide)
        qf = q.astype(F32)
        scores = []
        for s in range(steps):
            v = jnp.sum(qf * own_ref[s], axis=1, keepdims=True) * scale
            scores.append(jnp.where(step >= s, v, LOW))
        top = functools.reduce(jnp.maximum, scores)
        weights = [jnp.exp(v - top) for v in scores]
        all_w = functools.reduce(lambda a, b: a + b, weights)
        o = weights[0] * own_ref[0, :, :lat]
        for s in range(1, steps):
            o = o + weights[s] * own_ref[s, :, :lat]
        n_ref[:, h] = with_lse(o / all_w, top + jnp.log(all_w)).reshape(tiles, per, wide)


def queries(layer, tiles, scale, row_slot, q_nope, q_rope, w_uk, nk):
    steps, _, rows, _ = q_nope.shape
    _, heads, nope, lat = w_uk.shape
    wide = nk.shape[3]
    per = TILE_ROWS * steps
    shape = jax.ShapeDtypeStruct((tiles, heads, per, wide), BF)
    return pl.pallas_call(
        functools.partial(query_body, layer, steps, scale),
        grid=(heads // 2,),
        in_specs=[
            pl.BlockSpec(memory_space=pltpu.SMEM),
            pl.BlockSpec((steps, 1, rows, 2 * nope), lambda h: (0, layer, 0, h)),
            pl.BlockSpec((steps, 1, rows, 128), lambda h: (0, layer, 0, h)),
            pl.BlockSpec((1, 2, nope, lat), lambda h: (layer, h, 0, 0)),
            pl.BlockSpec((steps, 1, rows, wide), lambda h: (0, layer, 0, 0)),
        ],
        out_specs=[pl.BlockSpec((tiles, 2, per, wide), lambda h: (0, h, 0, 0))] * 2,
        out_shape=[shape, shape],
        scratch_shapes=[
            pltpu.VMEM((tiles * per, steps * rows), BF),
            pltpu.VMEM((steps, tiles * per, wide), F32),
        ],
        compiler_params=params(16),
        cost_estimate=cost(2 * tiles * per * heads * nope * lat, w_uk.size + 4 * tiles * per * heads * wide),
        name="queries",
    )(row_slot, q_nope, q_rope, w_uk, nk)


def attend_body(layer, scale, slot_ref, assign_ref, len_ref, qa_ref, qb_ref, *refs):
    pieces = refs[:4]
    ropes = refs[4:8] if layer else None
    oa_ref, ob_ref, keys, sems = refs[-4:]
    per_group = 2
    group = lax.axis_index("section")
    head = lax.axis_index("head")
    y = lax.div(head, jnp.int32(2))
    core = lax.rem(head, jnp.int32(2))
    tile = pl.program_id(0)
    wide = keys.shape[-1]
    lat = oa_ref.shape[3] - 128
    block = keys.shape[2] * keys.shape[3]
    _, heads, per, _ = qa_ref.shape
    count = heads * per

    @pl.when(tile == 0)
    def _():
        copies = []
        for k in range(4):
            at = lax.rem(y - k + 4, jnp.int32(4))
            for s in range(per_group):
                if layer == 0:
                    copies.append(pltpu.make_async_copy(pieces[k].at[:, s], keys.at[s, at], sems.at[k, s, 0]))
                else:
                    copies.append(pltpu.make_async_copy(
                        pieces[k].at[:, s], keys.at[s, at, :, :, pl.ds(0, lat)], sems.at[k, s, 0]))
                    copies.append(pltpu.make_async_copy(
                        ropes[k].at[:, s, :, pl.ds(lat, 128)], keys.at[s, at, :, :, pl.ds(lat, 128)], sems.at[k, s, 1]))
        for c in copies:
            c.start()
        for c in copies:
            c.wait()

    zeros = jnp.int32(slot_ref.shape[0])
    for r in range(slot_ref.shape[0]):
        zeros = zeros - slot_ref[r]
    tiles0 = lax.div(zeros + (TILE_ROWS - 1), jnp.int32(TILE_ROWS))
    tiles1 = lax.div(slot_ref.shape[0] - zeros + (TILE_ROWS - 1), jnp.int32(TILE_ROWS))
    slot = jnp.where(tile < tiles0, 0, 1)
    length = len_ref[assign_ref[group * per_group + slot]]
    blocks = lax.div(length - block * core + (2 * block - 1), jnp.int32(2 * block))
    blocks = jnp.where(tile < tiles0 + tiles1, jnp.clip(blocks, 0, 4), 0)
    factor = scale * math.log2(math.e)

    @pl.when(blocks == 0)
    def _():
        nothing = with_lse(jnp.zeros((count, lat), F32), jnp.full((count, 1), LOW, F32)).reshape(heads, per, wide)
        oa_ref[0] = nothing
        ob_ref[0] = nothing

    for n in range(1, 5):
        @pl.when(blocks == n)
        def _(n=n):
            left = length - (2 * (n - 1) + core) * block
            k = keys[slot, 0:n].reshape(n * block, wide)
            lane = lax.broadcasted_iota(jnp.int32, (count, block), 1)
            for q_ref, o_ref in ((qa_ref, oa_ref), (qb_ref, ob_ref)):
                q = q_ref[0].reshape(count, wide)
                s = lax.dot_general(q, k, (((1,), (1,)), ((), ())), preferred_element_type=F32)
                last = jnp.where(lane < left, s[:, (n - 1) * block:], LOW)
                s = last if n == 1 else jnp.concatenate([s[:, :(n - 1) * block], last], axis=1)
                top = jnp.max(s, axis=1, keepdims=True)
                p = jnp.exp2((s - top) * factor)
                total = jnp.sum(p, axis=1, keepdims=True)
                o = jnp.dot(p.astype(BF), k[:, :lat], preferred_element_type=F32)
                o_ref[0] = with_lse(o / total, top * scale + jnp.log(total)).reshape(heads, per, wide)


def attend(layer, scale, row_slot, assign, prompt_len, qa, qb, pieces, ropes):
    tiles, heads, per, wide = qa.shape
    parts, slots, rows, _ = pieces[0].shape
    spec = pl.BlockSpec((1, heads, per, wide), lambda i: (i, 0, 0, 0))
    smem = pl.BlockSpec(memory_space=pltpu.SMEM)
    held = list(pieces) + (list(ropes) if layer else [])
    shape = jax.ShapeDtypeStruct(qa.shape, BF)
    return pl.pallas_call(
        functools.partial(attend_body, layer, scale),
        grid=(tiles,),
        in_specs=[smem] * 3 + [spec] * 2 + [pl.BlockSpec(memory_space=pl.ANY)] * len(held),
        out_specs=[spec] * 2,
        out_shape=[shape, shape],
        scratch_shapes=[
            pltpu.VMEM((slots, 4, parts, rows, wide), BF),
            pltpu.SemaphoreType.DMA((4, slots, 2)),
        ],
        compiler_params=params(32),
        cost_estimate=cost(2 * 2 * tiles * heads * per * 4 * parts * rows * 1152, 4 * qa.size * 2, 0),
        name="attend",
    )(row_slot, assign, prompt_len, qa, qb, *held)


def merge_body(layer, steps, slot_ref, a_ref, b_ref, c_ref, w_ref, *refs):
    o_ref, back_ref = refs[-2:]
    tiles, heads, per, wide = a_ref.shape
    lat = wide - 128
    total = tiles * per
    rows = o_ref.shape[2]

    @pl.when(pl.program_id(0) == 0)
    def _():
        places, _, _ = row_places(slot_ref)
        sub = lax.broadcasted_iota(jnp.int32, (steps * rows, total), 0)
        step_of = sub // rows
        row_of = sub - step_of * rows
        where_to = jnp.full((steps * rows, total), -1, jnp.int32)
        for r in range(rows):
            where_to = jnp.where(row_of == r, places[r], where_to)
        place, step = order_index(1, (steps * rows, total), steps)
        back_ref[...] = jnp.where((place == where_to) & (step == step_of), 1.0, 0.0).astype(BF)

    back = back_ref[...]
    for h in range(heads):
        parts = [r[:, h].reshape(total, wide) for r in (a_ref, b_ref, c_ref)]
        lse = [jnp.sum(p[:, lat:].astype(F32), axis=1, keepdims=True) for p in parts]
        top = functools.reduce(jnp.maximum, lse)
        w = [jnp.exp(v - top) for v in lse]
        inv = 1.0 / (w[0] + w[1] + w[2])
        o = sum((wi * inv) * p[:, :lat].astype(F32) for wi, p in zip(w, parts))
        res = jnp.dot(o.astype(BF), w_ref[0, h], preferred_element_type=F32).astype(BF)
        res = jnp.dot(back, res, preferred_element_type=F32).astype(BF)
        value = res.shape[1]
        o_ref[:, 0, :, h * value:(h + 1) * value] = res.reshape(steps, rows, value)


def merge(layer, layers, steps, rows, row_slot, a, b, c, w_uv, before):
    tiles, heads, per, wide = a.shape
    lat, value = w_uv.shape[2:]
    spec = pl.BlockSpec((tiles, 2, per, wide), lambda h: (0, h, 0, 0))
    held = [] if before is None else [before]
    return pl.pallas_call(
        functools.partial(merge_body, layer, steps),
        grid=(heads // 2,),
        in_specs=[pl.BlockSpec(memory_space=pltpu.SMEM)] + [spec] * 3
        + [pl.BlockSpec((1, 2, lat, value), lambda h: (layer, h, 0, 0))]
        + [pl.BlockSpec(memory_space=pl.ANY)] * len(held),
        out_specs=pl.BlockSpec((steps, 1, rows, 2 * value), lambda h: (0, layer, 0, h)),
        out_shape=jax.ShapeDtypeStruct((steps, layers, rows, heads * value), BF),
        scratch_shapes=[pltpu.VMEM((steps * rows, tiles * per), BF)],
        input_output_aliases={5: 0} if held else {},
        compiler_params=params(16),
        cost_estimate=cost(2 * tiles * per * heads * lat * value, 3 * a.size * 2),
        name="merge",
    )(row_slot, a, b, c, w_uv, *held)


def local(n_section, n_head, kv_cache, prompt_len, assign, row_slot, q_nope, q_rope, new_kv, w_uk, w_uv):
    layers = kv_cache.shape[0]
    steps, _, rows, _ = q_nope.shape
    _, heads, nope, lat = w_uk.shape
    width = kv_cache.shape[3]
    rope = width - lat
    scale = (nope + rope) ** (-0.5)
    tiles = rows // TILE_ROWS + 1
    chips = n_head // 2

    def spread(x):
        return lax.all_to_all(x, "section", 0, 0, tiled=True)

    def along_y(x):
        out = [x]
        for k in range(1, chips):
            out.append(lax.ppermute(x, "head", [(h, ((h // 2 + k) % chips) * 2 + h % 2) for h in range(n_head)]))
        return out

    def swap(x):
        return lax.ppermute(x, "head", [(h, h ^ 1) for h in range(n_head)])

    x0, x1 = pack(kv_cache, n_section, lat)
    k0 = spread(pick(assign, spread(x0)))
    k1 = spread(pick(assign, spread(x1)))

    zero = jnp.zeros((steps, rows, rope), BF)
    nk = jnp.stack([
        jnp.concatenate([new_kv[:, 0], zero], axis=2),
        jnp.concatenate([new_kv[:, 1, :, :lat], zero, new_kv[:, 1, :, lat:]], axis=2),
    ], axis=1)
    qn = [queries(layer, tiles, scale, row_slot, q_nope, q_rope, w_uk, nk) for layer in range(layers)]
    sib = [swap(q) for q, _ in qn]

    p0 = along_y(k0)
    p1 = along_y(k1)
    out = None
    for layer, pieces in enumerate((p0, p1)):
        mine, theirs = attend(layer, scale, row_slot, assign, prompt_len, qn[layer][0], sib[layer], pieces, p0)
        out = merge(layer, layers, steps, rows, row_slot, mine, swap(theirs), qn[layer][1], w_uv, out)
    return out


def solution(mesh):
    in_specs = (
        P(None, "section", "head", None),
        P(),
        P(),
        P("section"),
        P(None, None, "section", "head"),
        P(None, None, "section", "head"),
        P(None, None, "section", None),
        P(None, "head", None, None),
        P(None, "head", None, None),
    )
    out_specs = P(None, None, "section", "head")
    step = functools.partial(local, mesh.shape["section"], mesh.shape["head"])
    return jax.shard_map(step, mesh=mesh, in_specs=in_specs, out_specs=out_specs, check_vma=False)
```

profile of v0, /device:TPU:39, one launch (start us, length us, event | category | flops | bytes accessed | tf_op | source)
XLA Modules:
  0.0 130.8 jit_solution(5498783879452589714)
XLA Ops:
  0.0 1.7 %copy.14.kv_ref = bf16[2,2,256,576]{3,2,1,0:T(8,128)(2,1)S(1)} copy(bf16[2,2,256,576]{2,3,1,0:T(8,128)(2,1)} %param.9) | data formatting | bytes 2359296 | tf_op args[0]
  1.7 1.1 pack.1
  2.8 0.8 copy-done.7
  3.7 7.4 %all-to-all-start.2 = ((bf16[16,2,16,640]{3,2,1,0:T(8,128)(2,1)}), bf16[16,2,16,640]{3,2,1,0:T(8,128)(2,1)S(1)}, u32[]{:S(2)}, u32[]{:S(2)}) async-start(bf16[16,2,16,640]{3,2,1,0:T(8,128)(2,1)} %copy-done.7), calls=%async_computation.2 | async-start | bytes 1310720 | tf_op jit(solution)/shard_map/all_to_all | solution.py:362
  11.3 2.2 %copy-done.1 = bf16[2,16,128,512]{3,2,1,0:T(8,128)(2,1)S(1)} copy-done((bf16[2,16,128,512]{3,2,1,0:T(8,128)(2,1)S(1)}, bf16[2,16,128,512]{3,2,1,0:T(8,128)(2,1)}, u32[]{:S(2)}) %copy-start.1) | copy-done | bytes 4194328
  13.5 6.2 %queries.3 = (bf16[5,16,16,640]{3,2,1,0:T(8,128)(2,1)}, bf16[5,16,16,640]{3,2,1,0:T(8,128)(2,1)S(1)}) custom-call(s32[32]{0:T(128)S(1)} %copy-done.8, bf16[2,2,32,2048]{3,2,1,0:T(8,128)(2,1)S(1)} %copy-done.3, bf16[2,2,32,1024]{3,2,1,0:T(8,128)(2,1)S(1)} %copy-done.6, bf16[2,16,128,512]{3,2,1,0:T(8,128)(2,1)S(1)} %copy-done.1, ...), custom_call_target="tpu_custom_call" | custom-call | flops 167772160 | bytes 5373952 | tf_op jit(solution)/shard_map/queries/pallas_call | solution.py:183
  19.7 1.2 collective-permute-start.8
  20.9 1.4 %pick.3 = bf16[32,16,640]{2,1,0:T(8,128)(2,1)} custom-call(s32[32]{0:T(128)S(1)} %copy-done.9, bf16[32,16,640]{2,1,0:T(8,128)(2,1)S(1)} %bitcast.20), custom_call_target="tpu_custom_call" | custom-call | bytes 1310720 | tf_op jit(solution)/shard_map/pick/pallas_call | solution.py:65
  22.3 6.7 %all-to-all-start.3 = ((bf16[16,2,16,640]{3,2,1,0:T(8,128)(2,1)}), bf16[16,2,16,640]{3,2,1,0:T(8,128)(2,1)}, u32[]{:S(2)}, u32[]{:S(2)}) async-start(bf16[16,2,16,640]{3,2,1,0:T(8,128)(2,1)} %bitcast.8), calls=%async_computation.3 | async-start | bytes 1310720 | tf_op jit(solution)/shard_map/all_to_all | solution.py:362
  29.0 2.2 %copy-done.2 = bf16[2,16,128,512]{3,2,1,0:T(8,128)(2,1)S(1)} copy-done((bf16[2,16,128,512]{3,2,1,0:T(8,128)(2,1)S(1)}, bf16[2,16,128,512]{3,2,1,0:T(8,128)(2,1)}, u32[]{:S(2)}) %copy-start.2) | copy-done | bytes 4194328
  31.2 6.2 %queries.2 = (bf16[5,16,16,640]{3,2,1,0:T(8,128)(2,1)}, bf16[5,16,16,640]{3,2,1,0:T(8,128)(2,1)S(1)}) custom-call(s32[32]{0:T(128)S(1)} %copy-done.8, bf16[2,2,32,2048]{3,2,1,0:T(8,128)(2,1)S(1)} %copy-done.3, bf16[2,2,32,1024]{3,2,1,0:T(8,128)(2,1)S(1)} %copy-done.6, bf16[2,16,128,512]{3,2,1,0:T(8,128)(2,1)S(1)} %copy-done.2, ...), custom_call_target="tpu_custom_call" | custom-call | flops 167772160 | bytes 5373952 | tf_op jit(solution)/shard_map/queries/pallas_call | solution.py:183
  37.4 1.2 copy-done.4
  38.6 1.8 %collective-permute-start = (bf16[5,16,16,640]{3,2,1,0:T(8,128)(2,1)}, bf16[5,16,16,640]{3,2,1,0:T(8,128)(2,1)}, u32[]{:S(2)}, u32[]{:S(2)}) collective-permute-start(bf16[5,16,16,640]{3,2,1,0:T(8,128)(2,1)} %get-tuple-element.15.qa_ref), channel_id=1, source_target_pairs={{0,1},{1,0},{2,3},{3,2},{4,5},{5,4},{6,7},{7,6},{8,9},{9,8},{10,11... | collective-permute-start | bytes 4915208 | tf_op jit(solution)/shard_map/ppermute | solution.py:371
  40.4 6.6 %all-to-all-start = ((bf16[16,2,16,512]{3,2,1,0:T(8,128)(2,1)}), bf16[16,2,16,512]{3,2,1,0:T(8,128)(2,1)S(1)}, u32[]{:S(2)}, u32[]{:S(2)}) async-start(bf16[16,2,16,512]{3,2,1,0:T(8,128)(2,1)} %get-tuple-element.16), calls=%async_computation | async-start | bytes 1048576 | tf_op jit(solution)/shard_map/all_to_all | solution.py:362
  47.1 2.7 %collective-permute-start.6 = (bf16[16,2,16,640]{3,2,1,0:T(8,128)(2,1)}, bf16[16,2,16,640]{3,2,1,0:T(8,128)(2,1)S(1)}, u32[]{:S(2)}, u32[]{:S(2)}) collective-permute-start(bf16[16,2,16,640]{3,2,1,0:T(8,128)(2,1)} %all-to-all-done.3.refs_4_.refs_0_), channel_id=1, source_target_pairs={{0,6},{1,7},{2,0},{3,1},{4,2},{5,3},{6,4},{7,5},{8,14},{9,15},{10,... | collective-permute-start | bytes 1966088 | tf_op jit(solution)/shard_map/ppermute | solution.py:367
  49.8 0.4 collective-permute-start.5
  50.2 0.7 collective-permute-start.4
  50.8 4.4 %all-to-all-done = bf16[16,2,16,512]{3,2,1,0:T(8,128)(2,1)S(1)} async-done(((bf16[16,2,16,512]{3,2,1,0:T(8,128)(2,1)}), bf16[16,2,16,512]{3,2,1,0:T(8,128)(2,1)S(1)}, u32[]{:S(2)}, u32[]{:S(2)}) %all-to-all-start) | async-done | bytes 524320 | tf_op jit(solution)/shard_map/all_to_all | solution.py:362
  55.2 0.6 pick.2
  55.8 13.7 %all_to_all.20.refs_0_ = bf16[16,2,16,512]{3,2,1,0:T(8,128)(2,1)S(1)} all-to-all(bf16[16,2,16,512]{3,2,1,0:T(8,128)(2,1)S(1)} %bitcast.22), channel_id=1, replica_groups=mesh['section'=16,'head'=8] {'section'}, dimensions={0} | all-to-all | bytes 1048576 | tf_op jit(solution)/shard_map/all_to_all | solution.py:362
  69.6 2.7 %collective-permute-start.3 = (bf16[16,2,16,512]{3,2,1,0:T(8,128)(2,1)S(1)}, bf16[16,2,16,512]{3,2,1,0:T(8,128)(2,1)S(1)}, u32[]{:S(2)}, u32[]{:S(2)}) collective-permute-start(bf16[16,2,16,512]{3,2,1,0:T(8,128)(2,1)S(1)} %all_to_all.20.refs_0_), channel_id=1, source_target_pairs={{0,6},{1,7},{2,0},{3,1},{4,2},{5,3},{6,4},{7,5},{8,14},{9,15},{10,... | collective-permute-start | bytes 1572872 | tf_op jit(solution)/shard_map/ppermute | solution.py:367
  72.3 4.3 %collective-permute-done.6.refs_7_.refs_3_ = bf16[16,2,16,640]{3,2,1,0:T(8,128)(2,1)S(1)} collective-permute-done((bf16[16,2,16,640]{3,2,1,0:T(8,128)(2,1)}, bf16[16,2,16,640]{3,2,1,0:T(8,128)(2,1)S(1)}, u32[]{:S(2)}, u32[]{:S(2)}) %collective-permute-start.6) | collective-permute-done | bytes 655392 | tf_op jit(solution)/shard_map/ppermute | solution.py:367
  76.6 4.5 %collective-permute-start.1 = (bf16[16,2,16,512]{3,2,1,0:T(8,128)(2,1)S(1)}, bf16[16,2,16,512]{3,2,1,0:T(8,128)(2,1)S(1)}, u32[]{:S(2)}, u32[]{:S(2)}) collective-permute-start(bf16[16,2,16,512]{3,2,1,0:T(8,128)(2,1)S(1)} %all_to_all.20.refs_0_), channel_id=1, source_target_pairs={{0,2},{1,3},{2,4},{3,5},{4,6},{5,7},{6,0},{7,1},{8,10},{9,11},{10,... | collective-permute-start | bytes 1572872 | tf_op jit(solution)/shard_map/ppermute | solution.py:367
  81.1 2.5 %collective-permute-done.4.refs_5_.refs_1_ = bf16[16,2,16,640]{3,2,1,0:T(8,128)(2,1)} collective-permute-done((bf16[16,2,16,640]{3,2,1,0:T(8,128)(2,1)}, bf16[16,2,16,640]{3,2,1,0:T(8,128)(2,1)}, u32[]{:S(2)}, u32[]{:S(2)}) %collective-permute-start.4) | collective-permute-done | bytes 655392 | tf_op jit(solution)/shard_map/ppermute | solution.py:367
  83.5 11.8 %attend.3 = (bf16[5,16,16,640]{3,2,1,0:T(8,128)(2,1)S(1)}, bf16[5,16,16,640]{3,2,1,0:T(8,128)(2,1)S(1)}) custom-call(s32[32]{0:T(128)S(1)} %copy-done.8, s32[32]{0:T(128)S(1)} %copy-done.9, s32[32]{0:T(128)S(1)} %copy-done.10, bf16[5,16,16,640]{3,2,1,0:T(8,128)(2,1)} %get-tuple-element.21.qa_ref, bf16[5,16,16,640]{3,2,1,0:T(8,128)(2,1)} %collective-permute-done.8.qb_ref, ...), custom_call_target="tpu_custom_call" | custom-call | flops 6039797760 | bytes 6553600 | tf_op jit(solution)/shard_map/attend/pallas_call | solution.py:281
  95.3 2.6 %collective-permute-start.9 = (bf16[5,16,16,640]{3,2,1,0:T(8,128)(2,1)S(1)}, bf16[5,16,16,640]{3,2,1,0:T(8,128)(2,1)S(1)}, u32[]{:S(2)}, u32[]{:S(2)}) collective-permute-start(bf16[5,16,16,640]{3,2,1,0:T(8,128)(2,1)S(1)} %get-tuple-element.23), channel_id=1, source_target_pairs={{0,1},{1,0},{2,3},{3,2},{4,5},{5,4},{6,7},{7,6},{8,9},{9,8},{10,11... | collective-permute-start | bytes 4915208 | tf_op jit(solution)/shard_map/ppermute | solution.py:371
  97.9 2.0 %collective-permute-done.3.refs_3_ = bf16[16,2,16,512]{3,2,1,0:T(8,128)(2,1)S(1)} collective-permute-done((bf16[16,2,16,512]{3,2,1,0:T(8,128)(2,1)S(1)}, bf16[16,2,16,512]{3,2,1,0:T(8,128)(2,1)S(1)}, u32[]{:S(2)}, u32[]{:S(2)}) %collective-permute-start.3) | collective-permute-done | bytes 524320 | tf_op jit(solution)/shard_map/ppermute | solution.py:367
  99.9 4.7 %collective-permute-done.1.refs_1_ = bf16[16,2,16,512]{3,2,1,0:T(8,128)(2,1)S(1)} collective-permute-done((bf16[16,2,16,512]{3,2,1,0:T(8,128)(2,1)S(1)}, bf16[16,2,16,512]{3,2,1,0:T(8,128)(2,1)S(1)}, u32[]{:S(2)}, u32[]{:S(2)}) %collective-permute-start.1) | collective-permute-done | bytes 524320 | tf_op jit(solution)/shard_map/ppermute | solution.py:367
  104.6 11.6 %attend.2 = (bf16[5,16,16,640]{3,2,1,0:T(8,128)(2,1)S(1)}, bf16[5,16,16,640]{3,2,1,0:T(8,128)(2,1)S(1)}) custom-call(s32[32]{0:T(128)S(1)} %copy-done.8, s32[32]{0:T(128)S(1)} %copy-done.9, s32[32]{0:T(128)S(1)} %copy-done.10, bf16[5,16,16,640]{3,2,1,0:T(8,128)(2,1)} %get-tuple-element.15.qa_ref, bf16[5,16,16,640]{3,2,1,0:T(8,128)(2,1)} %collective-permute-done.qb_ref, ...), custom_call_target="tpu_custom_call" | custom-call | flops 6039797760 | bytes 6553600 | tf_op jit(solution)/shard_map/attend/pallas_call | solution.py:281
  116.2 2.0 %collective-permute-start.7 = (bf16[5,16,16,640]{3,2,1,0:T(8,128)(2,1)S(1)}, bf16[5,16,16,640]{3,2,1,0:T(8,128)(2,1)S(1)}, u32[]{:S(2)}, u32[]{:S(2)}) collective-permute-start(bf16[5,16,16,640]{3,2,1,0:T(8,128)(2,1)S(1)} %get-tuple-element.19), channel_id=1, source_target_pairs={{0,1},{1,0},{2,3},{3,2},{4,5},{5,4},{6,7},{7,6},{8,9},{9,8},{10,11... | collective-permute-start | bytes 4915208 | tf_op jit(solution)/shard_map/ppermute | solution.py:371
  118.2 6.3 %merge.2.refs_0_ = bf16[2,2,32,2048]{3,2,1,0:T(8,128)(2,1)} custom-call(s32[32]{0:T(128)S(1)} %copy-done.8, bf16[5,16,16,640]{3,2,1,0:T(8,128)(2,1)S(1)} %get-tuple-element.22.a_ref, bf16[5,16,16,640]{3,2,1,0:T(8,128)(2,1)S(1)} %collective-permute-done.9.b_ref, bf16[5,16,16,640]{3,2,1,0:T(8,128)(2,1)S(1)} %get-tuple-element.24.c_ref, ...), custom_call_target="tpu_custom_call" | custom-call | flops 167772160 | bytes 4915200 | tf_op jit(solution)/shard_map/merge/pallas_call | solution.py:335
  124.5 6.3 %merge.3 = bf16[2,2,32,2048]{3,2,1,0:T(8,128)(2,1)} custom-call(s32[32]{0:T(128)S(1)} %copy-done.8, bf16[5,16,16,640]{3,2,1,0:T(8,128)(2,1)S(1)} %get-tuple-element.18.a_ref, bf16[5,16,16,640]{3,2,1,0:T(8,128)(2,1)S(1)} %collective-permute-done.7.b_ref, bf16[5,16,16,640]{3,2,1,0:T(8,128)(2,1)S(1)} %copy-done.5, ...), custom_call_target="tpu_custom_call", output_to_operand_aliasing={{}: (5, {})} | custom-call | flops 167772160 | bytes 4915200 | tf_op jit(solution)/shard_map/merge/pallas_call | solution.py:335
  (36 shorter events, 0.2 us)
Async XLA Ops:
  1.7 9.4 %copy-start.11 = (bf16[2,2,32,576]{3,2,1,0:T(8,128)(2,1)S(1)}, bf16[2,2,32,576]{3,2,1,0:T(8,128)(2,1)}, u32[]{:S(2)}) copy-start(bf16[2,2,32,576]{3,2,1,0:T(8,128)(2,1)} %param.15) | copy-start | bytes 442372
  1.7 9.5 %copy-start.3 = (bf16[2,2,32,2048]{3,2,1,0:T(8,128)(2,1)S(1)}, bf16[2,2,32,2048]{3,2,1,0:T(8,128)(2,1)}, u32[]{:S(2)}) copy-start(bf16[2,2,32,2048]{3,2,1,0:T(8,128)(2,1)} %nope_ref.3) | copy-start | bytes 1572868
  1.7 9.5 %copy-start.8 = (s32[32]{0:T(128)S(1)}, s32[32]{0:T(128)}, u32[]{:S(2)}) copy-start(s32[32]{0:T(128)} %slot_ref.11) | copy-start | bytes 388
  2.8 0.8 copy-start.7
  3.7 7.6 %copy-start.6 = (bf16[2,2,32,1024]{3,2,1,0:T(8,128)(2,1)S(1)}, bf16[2,2,32,1024]{3,2,1,0:T(8,128)(2,1)}, u32[]{:S(2)}) copy-start(bf16[2,2,32,1024]{3,2,1,0:T(8,128)(2,1)} %rope_ref.3) | copy-start | bytes 786436
  3.7 17.2 %all-to-all-start.2 = ((bf16[16,2,16,640]{3,2,1,0:T(8,128)(2,1)}), bf16[16,2,16,640]{3,2,1,0:T(8,128)(2,1)S(1)}, u32[]{:S(2)}, u32[]{:S(2)}) async-start(bf16[16,2,16,640]{3,2,1,0:T(8,128)(2,1)} %copy-done.7), calls=%async_computation.2 | async-start | bytes 1310720 | tf_op jit(solution)/shard_map/all_to_all | solution.py:362
  11.3 2.2 %copy-start.1 = (bf16[2,16,128,512]{3,2,1,0:T(8,128)(2,1)S(1)}, bf16[2,16,128,512]{3,2,1,0:T(8,128)(2,1)}, u32[]{:S(2)}) copy-start(bf16[2,16,128,512]{3,2,1,0:T(8,128)(2,1)} %w_ref.5) | copy-start | bytes 12582916
  13.5 7.4 %copy-start.9 = (s32[32]{0:T(128)S(1)}, s32[32]{0:T(128)}, u32[]{:S(2)}) copy-start(s32[32]{0:T(128)} %assign_ref.7) | copy-start | bytes 388
  19.7 49.9 %collective-permute-start.8 = (bf16[5,16,16,640]{3,2,1,0:T(8,128)(2,1)}, bf16[5,16,16,640]{3,2,1,0:T(8,128)(2,1)}, u32[]{:S(2)}, u32[]{:S(2)}) collective-permute-start(bf16[5,16,16,640]{3,2,1,0:T(8,128)(2,1)} %get-tuple-element.21.qa_ref), channel_id=1, source_target_pairs={{0,1},{1,0},{2,3},{3,2},{4,5},{5,4},{6,7},{7,6},{8,9},{9,8},{10,11... | collective-permute-start | bytes 4915208 | tf_op jit(solution)/shard_map/ppermute | solution.py:371
  22.3 18.1 %all-to-all-start.3 = ((bf16[16,2,16,640]{3,2,1,0:T(8,128)(2,1)}), bf16[16,2,16,640]{3,2,1,0:T(8,128)(2,1)}, u32[]{:S(2)}, u32[]{:S(2)}) async-start(bf16[16,2,16,640]{3,2,1,0:T(8,128)(2,1)} %bitcast.8), calls=%async_computation.3 | async-start | bytes 1310720 | tf_op jit(solution)/shard_map/all_to_all | solution.py:362
  29.0 2.2 %copy-start.2 = (bf16[2,16,128,512]{3,2,1,0:T(8,128)(2,1)S(1)}, bf16[2,16,128,512]{3,2,1,0:T(8,128)(2,1)}, u32[]{:S(2)}) copy-start(bf16[2,16,128,512]{3,2,1,0:T(8,128)(2,1)} %w_ref.5) | copy-start | bytes 12582916
  37.4 1.2 copy-start.4
  38.6 44.9 %copy-start.10 = (s32[32]{0:T(128)S(1)}, s32[32]{0:T(128)}, u32[]{:S(2)}) copy-start(s32[32]{0:T(128)} %len_ref.3) | copy-start | bytes 388
  38.6 66.0 %collective-permute-start = (bf16[5,16,16,640]{3,2,1,0:T(8,128)(2,1)}, bf16[5,16,16,640]{3,2,1,0:T(8,128)(2,1)}, u32[]{:S(2)}, u32[]{:S(2)}) collective-permute-start(bf16[5,16,16,640]{3,2,1,0:T(8,128)(2,1)} %get-tuple-element.15.qa_ref), channel_id=1, source_target_pairs={{0,1},{1,0},{2,3},{3,2},{4,5},{5,4},{6,7},{7,6},{8,9},{9,8},{10,11... | collective-permute-start | bytes 4915208 | tf_op jit(solution)/shard_map/ppermute | solution.py:371
  40.4 14.8 %all-to-all-start = ((bf16[16,2,16,512]{3,2,1,0:T(8,128)(2,1)}), bf16[16,2,16,512]{3,2,1,0:T(8,128)(2,1)S(1)}, u32[]{:S(2)}, u32[]{:S(2)}) async-start(bf16[16,2,16,512]{3,2,1,0:T(8,128)(2,1)} %get-tuple-element.16), calls=%async_computation | async-start | bytes 1048576 | tf_op jit(solution)/shard_map/all_to_all | solution.py:362
  47.1 29.5 %collective-permute-start.6 = (bf16[16,2,16,640]{3,2,1,0:T(8,128)(2,1)}, bf16[16,2,16,640]{3,2,1,0:T(8,128)(2,1)S(1)}, u32[]{:S(2)}, u32[]{:S(2)}) collective-permute-start(bf16[16,2,16,640]{3,2,1,0:T(8,128)(2,1)} %all-to-all-done.3.refs_4_.refs_0_), channel_id=1, source_target_pairs={{0,6},{1,7},{2,0},{3,1},{4,2},{5,3},{6,4},{7,5},{8,14},{9,15},{10,... | collective-permute-start | bytes 1966088 | tf_op jit(solution)/shard_map/ppermute | solution.py:367
  49.8 26.8 %collective-permute-start.5 = (bf16[16,2,16,640]{3,2,1,0:T(8,128)(2,1)}, bf16[16,2,16,640]{3,2,1,0:T(8,128)(2,1)}, u32[]{:S(2)}, u32[]{:S(2)}) collective-permute-start(bf16[16,2,16,640]{3,2,1,0:T(8,128)(2,1)} %all-to-all-done.3.refs_4_.refs_0_), channel_id=1, source_target_pairs={{0,4},{1,5},{2,6},{3,7},{4,0},{5,1},{6,2},{7,3},{8,12},{9,13},{10,... | collective-permute-start | bytes 1966088 | tf_op jit(solution)/shard_map/ppermute | solution.py:367
  50.2 33.4 %collective-permute-start.4 = (bf16[16,2,16,640]{3,2,1,0:T(8,128)(2,1)}, bf16[16,2,16,640]{3,2,1,0:T(8,128)(2,1)}, u32[]{:S(2)}, u32[]{:S(2)}) collective-permute-start(bf16[16,2,16,640]{3,2,1,0:T(8,128)(2,1)} %all-to-all-done.3.refs_4_.refs_0_), channel_id=1, source_target_pairs={{0,2},{1,3},{2,4},{3,5},{4,6},{5,7},{6,0},{7,1},{8,10},{9,11},{10,... | collective-permute-start | bytes 1966088 | tf_op jit(solution)/shard_map/ppermute | solution.py:367
  69.6 30.3 %collective-permute-start.3 = (bf16[16,2,16,512]{3,2,1,0:T(8,128)(2,1)S(1)}, bf16[16,2,16,512]{3,2,1,0:T(8,128)(2,1)S(1)}, u32[]{:S(2)}, u32[]{:S(2)}) collective-permute-start(bf16[16,2,16,512]{3,2,1,0:T(8,128)(2,1)S(1)} %all_to_all.20.refs_0_), channel_id=1, source_target_pairs={{0,6},{1,7},{2,0},{3,1},{4,2},{5,3},{6,4},{7,5},{8,14},{9,15},{10,... | collective-permute-start | bytes 1572872 | tf_op jit(solution)/shard_map/ppermute | solution.py:367
  76.6 23.3 %collective-permute-start.2 = (bf16[16,2,16,512]{3,2,1,0:T(8,128)(2,1)S(1)}, bf16[16,2,16,512]{3,2,1,0:T(8,128)(2,1)S(1)}, u32[]{:S(2)}, u32[]{:S(2)}) collective-permute-start(bf16[16,2,16,512]{3,2,1,0:T(8,128)(2,1)S(1)} %all_to_all.20.refs_0_), channel_id=1, source_target_pairs={{0,4},{1,5},{2,6},{3,7},{4,0},{5,1},{6,2},{7,3},{8,12},{9,13},{10,... | collective-permute-start | bytes 1572872 | tf_op jit(solution)/shard_map/ppermute | solution.py:367
  76.6 28.0 %collective-permute-start.1 = (bf16[16,2,16,512]{3,2,1,0:T(8,128)(2,1)S(1)}, bf16[16,2,16,512]{3,2,1,0:T(8,128)(2,1)S(1)}, u32[]{:S(2)}, u32[]{:S(2)}) collective-permute-start(bf16[16,2,16,512]{3,2,1,0:T(8,128)(2,1)S(1)} %all_to_all.20.refs_0_), channel_id=1, source_target_pairs={{0,2},{1,3},{2,4},{3,5},{4,6},{5,7},{6,0},{7,1},{8,10},{9,11},{10,... | collective-permute-start | bytes 1572872 | tf_op jit(solution)/shard_map/ppermute | solution.py:367
  95.3 22.9 %collective-permute-start.9 = (bf16[5,16,16,640]{3,2,1,0:T(8,128)(2,1)S(1)}, bf16[5,16,16,640]{3,2,1,0:T(8,128)(2,1)S(1)}, u32[]{:S(2)}, u32[]{:S(2)}) collective-permute-start(bf16[5,16,16,640]{3,2,1,0:T(8,128)(2,1)S(1)} %get-tuple-element.23), channel_id=1, source_target_pairs={{0,1},{1,0},{2,3},{3,2},{4,5},{5,4},{6,7},{7,6},{8,9},{9,8},{10,11... | collective-permute-start | bytes 4915208 | tf_op jit(solution)/shard_map/ppermute | solution.py:371
  104.6 13.6 %copy-start = (bf16[2,16,512,128]{3,2,1,0:T(8,128)(2,1)S(1)}, bf16[2,16,512,128]{3,2,1,0:T(8,128)(2,1)}, u32[]{:S(2)}) copy-start(bf16[2,16,512,128]{3,2,1,0:T(8,128)(2,1)} %w_ref.7) | copy-start | bytes 12582916
  116.2 8.3 %collective-permute-start.7 = (bf16[5,16,16,640]{3,2,1,0:T(8,128)(2,1)S(1)}, bf16[5,16,16,640]{3,2,1,0:T(8,128)(2,1)S(1)}, u32[]{:S(2)}, u32[]{:S(2)}) collective-permute-start(bf16[5,16,16,640]{3,2,1,0:T(8,128)(2,1)S(1)} %get-tuple-element.19), channel_id=1, source_target_pairs={{0,1},{1,0},{2,3},{3,2},{4,5},{5,4},{6,7},{7,6},{8,9},{9,8},{10,11... | collective-permute-start | bytes 4915208 | tf_op jit(solution)/shard_map/ppermute | solution.py:371
  118.2 6.3 %copy-start.5 = (bf16[5,16,16,640]{3,2,1,0:T(8,128)(2,1)S(1)}, bf16[5,16,16,640]{3,2,1,0:T(8,128)(2,1)}, u32[]{:S(2)}) copy-start(bf16[5,16,16,640]{3,2,1,0:T(8,128)(2,1)} %copy-done.4) | copy-start | bytes 4915204
where the time goes:
time: 132 us; the launch traced here: 131 us
  Pallas kernels  51.5 us (39%)
  starting transfers between devices  39.3 us (30%)
  waiting for transfers between devices  17.8 us (13%)
  blocking collectives  13.7 us (10%)
  local copies, waits for them, and re-layouts  8.15 us (6%)
    pallas_call x2, Pallas kernels, attend(): pl.pallas_call(functools.partial(attend_body, layer, scale), grid=(tiles,...  23.4 us
    all_to_all x3, starting transfers between devices, spread(): return lax.all_to_all(x, 'section', 0, 0, tiled=True)  20.7 us
    all_to_all x1, blocking collectives, spread(): return lax.all_to_all(x, 'section', 0, 0, tiled=True)  13.7 us
    ppermute x6, waiting for transfers between devices, along_y(): lax.ppermute(x, 'head', [(h, (h // 2 + k) % chips * 2 + h % 2) for h in r...  13.4 us
    pallas_call x2, Pallas kernels, merge(): pl.pallas_call(functools.partial(merge_body, layer, steps), grid=(heads /...  12.6 us
    pallas_call x2, Pallas kernels, queries(): pl.pallas_call(functools.partial(query_body, layer, steps, scale), grid=(...  12.4 us
    ppermute x6, starting transfers between devices, along_y(): lax.ppermute(x, 'head', [(h, (h // 2 + k) % chips * 2 + h % 2) for h in r...  11 us
    unnamed x25, local copies, waits for them, and re-layouts  8.12 us
  transfers between devices with their start and end apart: 13, of which 5 were waited for; matrix products, arithmetic and copies ran while one was open for 0% of the time, Pallas kernels for 34%

commit v1 on v0

v1 whole, which is shorter than its diff:
```python
import functools
import math

import jax
import jax.numpy as jnp
from jax import lax
from jax.experimental import pallas as pl
from jax.experimental.pallas import tpu as pltpu
from jax.sharding import PartitionSpec as P

BF = jnp.bfloat16
F32 = jnp.float32
TILE_ROWS = 8
LOW = -1e30
MIB = 1 << 20


def params(limit, **extra):
    return pltpu.CompilerParams(vmem_limit_bytes=limit * MIB, **extra)


def cost(flops, nbytes, trans=0):
    return pl.CostEstimate(flops=int(flops), bytes_accessed=int(nbytes), transcendentals=int(trans))


def pack_body(lat, kv_ref, x_ref):
    parts, _, rows, wide = x_ref.shape
    a = kv_ref[0, 0].T
    b = kv_ref[1, 0].T
    x = jnp.concatenate([a[:, :lat], b[:, :lat], a[:, lat:], b[:, lat:]], axis=1)
    x_ref[:, 0] = x.reshape(parts, rows, wide)


def pack(kv, parts, lat):
    layers, prompts, tok, width = kv.shape
    rows = tok // parts
    return pl.pallas_call(
        functools.partial(pack_body, lat),
        grid=(prompts,),
        in_specs=[pl.BlockSpec((layers, 1, width, tok), lambda p: (0, p, 0, 0))],
        out_specs=pl.BlockSpec((parts, 1, rows, layers * width), lambda p: (0, p, 0, 0)),
        out_shape=jax.ShapeDtypeStruct((parts, prompts, rows, layers * width), BF),
        compiler_params=params(16),
        cost_estimate=cost(0, 2 * kv.size * 2),
        name="pack",
    )(kv.transpose(0, 1, 3, 2))


def pick_body(layer, lat, assign_ref, x_ref, o_ref):
    for i in range(o_ref.shape[0]):
        p = assign_ref[i]
        o_ref[i, :, :lat] = x_ref[p, :, layer * lat:(layer + 1) * lat]
        if layer == 0:
            o_ref[i, :, lat:] = x_ref[p, :, 2 * lat:]


def pick(layer, lat, assign, x):
    groups, slots, rows, wide = x.shape
    out = lat if layer else wide - lat
    res = pl.pallas_call(
        functools.partial(pick_body, layer, lat),
        in_specs=[
            pl.BlockSpec(memory_space=pltpu.SMEM),
            pl.BlockSpec(memory_space=pltpu.VMEM),
        ],
        out_specs=pl.BlockSpec(memory_space=pltpu.VMEM),
        out_shape=jax.ShapeDtypeStruct((groups * slots, rows, out), BF),
        compiler_params=params(16),
        cost_estimate=cost(0, 2 * x.size * 2),
        name="pick",
    )(assign, x.reshape(groups * slots, rows, wide))
    return res.reshape(groups, slots, rows, out)


def count_zeros(slot_ref):
    zeros = jnp.int32(slot_ref.shape[0])
    for r in range(slot_ref.shape[0]):
        zeros = zeros - slot_ref[r]
    return zeros


def row_places(slot_ref):
    places = []
    c0, c1 = jnp.int32(0), count_zeros(slot_ref)
    for r in range(slot_ref.shape[0]):
        s = slot_ref[r]
        places.append(jnp.where(s == 0, c0, c1))
        c0 = c0 + (1 - s)
        c1 = c1 + s
    return places


def order_index(axis, shape, steps):
    i = lax.broadcasted_iota(jnp.int32, shape, axis)
    per = TILE_ROWS * steps
    tile = i // per
    rest = i - tile * per
    step = rest // TILE_ROWS
    return tile * TILE_ROWS + (rest - step * TILE_ROWS), step


def split2(x):
    hi = x.astype(BF).astype(F32)
    return hi, (x - hi).astype(BF).astype(F32)


def partial_of(o, top, total):
    lane = lax.broadcasted_iota(jnp.int32, (o.shape[0], 128), 1)
    tail = jnp.zeros((o.shape[0], 128), F32)
    for i, v in enumerate(top + total):
        tail = jnp.where(lane == i, v, tail)
    return jnp.concatenate([o, tail], axis=1)


def query_body(layer, steps, scale, slot_ref, nope_ref, rope_ref, w_ref, nk_ref, q_ref, n_ref, perm_ref, own_ref):
    tiles, heads, per, wide = q_ref.shape
    rows = nope_ref.shape[2]
    nope = w_ref.shape[2]
    lat = w_ref.shape[3]
    total = tiles * per

    @pl.when(pl.program_id(0) == 0)
    def _():
        places = row_places(slot_ref)
        lane = lax.broadcasted_iota(jnp.int32, (1, steps * rows), 1)
        step_of = lane // rows
        row_of = lane - step_of * rows
        where_to = jnp.full((1, steps * rows), -1, jnp.int32)
        for r in range(rows):
            where_to = jnp.where(row_of == r, places[r], where_to)
        place, step = order_index(0, (total, steps * rows), steps)
        perm_ref[...] = jnp.where((place == where_to) & (step == step_of), 1.0, 0.0).astype(BF)
        lane1 = lax.broadcasted_iota(jnp.int32, (total, rows), 1)
        place1, _ = order_index(0, (total, rows), steps)
        where1 = jnp.full((1, rows), -1, jnp.int32)
        lane_r = lax.broadcasted_iota(jnp.int32, (1, rows), 1)
        for r in range(rows):
            where1 = jnp.where(lane_r == r, places[r], where1)
        by_row = jnp.where(place1 == where1, 1.0, 0.0).astype(BF)
        for s in range(steps):
            own_ref[s] = jnp.dot(by_row, nk_ref[s, 0], preferred_element_type=F32)

    perm = perm_ref[...]
    x = nope_ref[:, 0].reshape(steps * rows, heads * nope)
    x = jnp.dot(perm, x, preferred_element_type=F32).astype(BF)
    r = rope_ref[:, 0].reshape(steps * rows, 128)
    r = jnp.dot(perm, r, preferred_element_type=F32)
    rolled = pltpu.roll(r, 64, 1)
    lane = lax.broadcasted_iota(jnp.int32, (total, 128), 1)
    mine = (lane // 64) == layer
    _, step = order_index(0, (total, 1), steps)
    for h in range(heads):
        ql = jnp.dot(x[:, h * nope:(h + 1) * nope], w_ref[0, h], preferred_element_type=F32).astype(BF)
        qr = jnp.where(mine, r if h == layer else rolled, 0.0).astype(BF)
        q = jnp.concatenate([ql, qr], axis=1)
        q_ref[:, h] = q.reshape(tiles, per, wide)
        qf = q.astype(F32)
        scores = []
        for s in range(steps):
            v = jnp.sum(qf * own_ref[s], axis=1, keepdims=True) * scale
            scores.append(jnp.where(step >= s, v, LOW))
        top = split2(functools.reduce(jnp.maximum, scores))
        weights = [jnp.exp(v - (top[0] + top[1])) for v in scores]
        o = weights[0] * own_ref[0, :, :lat]
        for s in range(1, steps):
            o = o + weights[s] * own_ref[s, :, :lat]
        part = partial_of(o, top, split2(sum(weights)))
        n_ref[:, h] = part.astype(BF).reshape(tiles, per, wide)


def queries(layer, tiles, scale, row_slot, q_nope, q_rope, w_uk, nk):
    steps, _, rows, _ = q_nope.shape
    _, heads, nope, lat = w_uk.shape
    wide = nk.shape[3]
    per = TILE_ROWS * steps
    shape = jax.ShapeDtypeStruct((tiles, heads, per, wide), BF)
    return pl.pallas_call(
        functools.partial(query_body, layer, steps, scale),
        grid=(heads // 2,),
        in_specs=[
            pl.BlockSpec(memory_space=pltpu.SMEM),
            pl.BlockSpec((steps, 1, rows, 2 * nope), lambda h: (0, layer, 0, h)),
            pl.BlockSpec((steps, 1, rows, 128), lambda h: (0, layer, 0, h)),
            pl.BlockSpec((1, 2, nope, lat), lambda h: (layer, h, 0, 0)),
            pl.BlockSpec((steps, 1, rows, wide), lambda h: (0, layer, 0, 0)),
        ],
        out_specs=[pl.BlockSpec((tiles, 2, per, wide), lambda h: (0, h, 0, 0))] * 2,
        out_shape=[shape, shape],
        scratch_shapes=[
            pltpu.VMEM((tiles * per, steps * rows), BF),
            pltpu.VMEM((steps, tiles * per, wide), F32),
        ],
        compiler_params=params(16),
        cost_estimate=cost(2 * tiles * per * heads * nope * lat, w_uk.size + 4 * tiles * per * heads * wide),
        name="queries",
    )(row_slot, q_nope, q_rope, w_uk, nk)


def attend_body(layer, scale, shifts, slot_ref, assign_ref, len_ref, qa_ref, qb_ref, *refs):
    names = [(k, i) for k in shifts for i in range(2 if k == 2 else 1)]
    pieces = refs[:len(names)]
    ropes = refs[len(names):2 * len(names)] if layer else None
    oa_ref, ob_ref, keys, sems = refs[-4:]
    slots = keys.shape[0]
    group = lax.axis_index("section")
    head = lax.axis_index("head")
    y = lax.div(head, jnp.int32(2))
    core = lax.rem(head, jnp.int32(2))
    wide = keys.shape[-1]
    lat = wide - 128
    block = keys.shape[2] * keys.shape[3]
    tiles, heads, per, _ = qa_ref.shape
    count = heads * per
    half = keys.shape[2] // 2
    own = lat if layer else wide
    origin = {k: lax.rem(y - k + 4, jnp.int32(4)) for k in shifts}

    def copies(s):
        out = []
        for j, (k, i) in enumerate(names):
            at = sum(jnp.where(origin[o] < origin[k], 1, 0) for o in shifts)
            to = pl.ds(i * half, half) if k == 2 else pl.ds(0, 2 * half)
            out.append(pltpu.make_async_copy(
                pieces[j].at[:, s], keys.at[s, at, to, :, pl.ds(0, own)], sems.at[k, s, i]))
            if layer:
                out.append(pltpu.make_async_copy(
                    ropes[j].at[:, s, :, pl.ds(lat, 128)], keys.at[s, at, to, :, pl.ds(lat, 128)],
                    sems.at[k, s, 2 + i]))
        return out

    moving = [copies(s) for s in range(slots)]
    for group_of in moving:
        for c in group_of:
            c.start()
    for group_of in moving:
        for c in group_of:
            c.wait()
    zeros = count_zeros(slot_ref)
    factor = scale * math.log2(math.e)

    def put(o_ref, tile, slot, r):
        i = lax.broadcasted_iota(jnp.int32, (count, 1), 0)
        row = tile * TILE_ROWS + lax.rem(i, jnp.int32(TILE_ROWS))
        before = o_ref[tile].reshape(count, wide).astype(F32)
        o_ref[tile] = jnp.where((slot == 1) & (row < zeros), before, r).astype(BF).reshape(heads, per, wide)

    def chains(todo, slot, n, left):
        k = keys[slot, 0:n].reshape(n * block, wide)
        lane = lax.broadcasted_iota(jnp.int32, (count, block), 1)
        jobs = [(tile, q_ref, o_ref) for tile in todo for q_ref, o_ref in ((qa_ref, oa_ref), (qb_ref, ob_ref))]

        def scores_of(job):
            return lax.dot_general(
                job[1][job[0]].reshape(count, wide), k, (((1,), (1,)), ((), ())), preferred_element_type=F32)

        ahead = [scores_of(job) for job in jobs[:2]]
        for i, (tile, _, o_ref) in enumerate(jobs):
            if i + 2 < len(jobs):
                ahead.append(scores_of(jobs[i + 2]))
            s = ahead[i]
            last = jnp.where(lane < left, s[:, (n - 1) * block:], LOW)
            s = last if n == 1 else jnp.concatenate([s[:, :(n - 1) * block], last], axis=1)
            top = split2(jnp.max(s, axis=1, keepdims=True) * scale)
            p = jnp.exp2(s * factor - (top[0] + top[1]) * math.log2(math.e))
            total = jnp.sum(p, axis=1, keepdims=True)
            o = jnp.dot(p.astype(BF), k[:, :lat], preferred_element_type=F32)
            put(o_ref, tile, slot, partial_of(o, top, split2(total)))

    def one_slot(slot, carry):
        begin = jnp.where(slot == 0, 0, lax.div(zeros, jnp.int32(TILE_ROWS)))
        end = jnp.where(slot == 0, lax.div(zeros + (TILE_ROWS - 1), jnp.int32(TILE_ROWS)), tiles)
        length = len_ref[assign_ref[group * slots + slot]]
        prefix = lax.div(length - block * core + (2 * block - 1), jnp.int32(2 * block))
        blocks = sum(jnp.where(origin[k] < prefix, 1, 0) for k in shifts)
        final = functools.reduce(jnp.maximum, [jnp.where(origin[k] < prefix, origin[k], 0) for k in shifts])
        left = length - (2 * final + core) * block
        pairs = lax.div(end - begin, jnp.int32(2))

        @pl.when(blocks == 0)
        def _():
            nothing = partial_of(jnp.zeros((count, lat), F32), (jnp.full((count, 1), LOW, F32),), ())

            def fill(tile, c):
                put(oa_ref, tile, slot, nothing)
                put(ob_ref, tile, slot, nothing)
                return c

            lax.fori_loop(begin, end, fill, 0)

        for n in range(1, len(shifts) + 1):
            @pl.when(blocks == n)
            def _(n=n):
                def pair(i, c):
                    chains([begin + 2 * i, begin + 2 * i + 1], slot, n, left)
                    return c

                lax.fori_loop(0, pairs, pair, 0)

                @pl.when(begin + 2 * pairs < end)
                def _():
                    chains([end - 1], slot, n, left)
        return carry

    lax.fori_loop(0, slots, one_slot, 0)


def attend(layer, scale, shifts, row_slot, assign, prompt_len, qa, qb, pieces, ropes):
    tiles, heads, per, wide = qa.shape
    parts, slots, rows, _ = ropes[0].shape
    smem = pl.BlockSpec(memory_space=pltpu.SMEM)
    vmem = pl.BlockSpec(memory_space=pltpu.VMEM)
    held = list(pieces) + (list(ropes) if layer else [])
    shape = jax.ShapeDtypeStruct(qa.shape, BF)
    part = len(shifts)
    parts = parts if 2 not in shifts or part > 1 else 2 * parts
    return pl.pallas_call(
        functools.partial(attend_body, layer, scale, shifts),
        in_specs=[smem] * 3 + [vmem] * 2 + [pl.BlockSpec(memory_space=pl.ANY)] * len(held),
        out_specs=[vmem] * 2,
        out_shape=[shape, shape],
        scratch_shapes=[
            pltpu.VMEM((slots, part, parts, rows, wide), BF),
            pltpu.SemaphoreType.DMA((4, slots, 4)),
        ],
        compiler_params=params(32),
        cost_estimate=cost(2 * 2 * tiles * heads * per * part * parts * rows * 1152, 4 * qa.size * 2, 0),
        name="attend",
    )(row_slot, assign, prompt_len, qa, qb, *held)


def merge_body(layer, steps, count, slot_ref, w_ref, *refs):
    o_ref = refs[-1]
    partials = refs[:count]
    tiles, heads, per, wide = partials[0].shape
    lat = wide - 128
    total = tiles * per
    rows = o_ref.shape[2]
    value = w_ref.shape[3]

    places = row_places(slot_ref)
    sub = lax.broadcasted_iota(jnp.int32, (steps * rows, total), 0)
    step_of = sub // rows
    row_of = sub - step_of * rows
    where_to = jnp.full((steps * rows, total), -1, jnp.int32)
    for r in range(rows):
        where_to = jnp.where(row_of == r, places[r], where_to)
    place, step = order_index(1, (steps * rows, total), steps)
    back = jnp.where((place == where_to) & (step == step_of), 1.0, 0.0).astype(BF)

    lane = lax.broadcasted_iota(jnp.int32, (128, 128), 0)
    spread_top = jnp.where(lane < 2, 1.0, 0.0).astype(BF)
    spread_total = jnp.where((lane >= 2) & (lane < 4), 1.0, 0.0).astype(BF)
    every = tiles * heads * per
    tails = [r[:, :, :, lat:].reshape(every, 128) for r in partials]
    tops = [jnp.dot(v, spread_top, preferred_element_type=F32) for v in tails]
    totals = [jnp.dot(v, spread_total, preferred_element_type=F32) for v in tails]
    top = functools.reduce(jnp.maximum, tops)
    w = [jnp.exp(v - top) for v in tops]
    inv = 1.0 / sum(wi * v for wi, v in zip(w, totals))
    w = [wi * inv for wi in w]
    o = jnp.concatenate([
        sum(wi * r[:, :, :, c:c + 128].reshape(every, 128).astype(F32) for wi, r in zip(w, partials)).astype(BF)
        for c in range(0, lat, 128)
    ], axis=1).reshape(tiles, heads, per, lat)
    res = [
        jnp.dot(o[:, h].reshape(total, lat), w_ref[layer, h], preferred_element_type=F32).astype(BF)
        for h in range(heads)
    ]
    res = jnp.dot(back, jnp.concatenate(res, axis=1), preferred_element_type=F32).astype(BF)
    o_ref[:, 0] = res.reshape(steps, rows, heads * value)


def merge(layer, layers, steps, rows, row_slot, partials, w_uv, before):
    tiles, heads, per, wide = partials[0].shape
    lat, value = w_uv.shape[2:]
    vmem = pl.BlockSpec(memory_space=pltpu.VMEM)
    held = [] if before is None else [before]
    return pl.pallas_call(
        functools.partial(merge_body, layer, steps, len(partials)),
        grid=(1,),
        in_specs=[pl.BlockSpec(memory_space=pltpu.SMEM)] + [vmem] * (1 + len(partials))
        + [pl.BlockSpec(memory_space=pl.ANY)] * len(held),
        out_specs=pl.BlockSpec((steps, 1, rows, heads * value), lambda i: (0, layer, 0, 0)),
        out_shape=jax.ShapeDtypeStruct((steps, layers, rows, heads * value), BF),
        input_output_aliases={2 + len(partials): 0} if held else {},
        compiler_params=params(24),
        cost_estimate=cost(2 * tiles * per * heads * lat * value, len(partials) * partials[0].size * 2),
        name="merge",
    )(row_slot, w_uv, *partials, *held)


def local(n_section, n_head, kv_cache, prompt_len, assign, row_slot, q_nope, q_rope, new_kv, w_uk, w_uv):
    layers = kv_cache.shape[0]
    steps, _, rows, _ = q_nope.shape
    _, heads, nope, lat = w_uk.shape
    width = kv_cache.shape[3]
    rope = width - lat
    scale = (nope + rope) ** (-0.5)
    tiles = rows // TILE_ROWS
    chips = n_head // 2

    def spread(x):
        return lax.all_to_all(x, "section", 0, 0, tiled=True)

    def step_y(x, k):
        return lax.ppermute(x, "head", [(h, ((h // 2 + k) % chips) * 2 + h % 2) for h in range(n_head)])

    def onward(up, down):
        half = up.shape[0] // 2
        return [step_y(up[:half], 1), step_y(down[half:], -1)]

    def swap(x):
        return lax.ppermute(x, "head", [(h, h ^ 1) for h in range(n_head)])

    zero = jnp.zeros((steps, rows, rope), BF)
    nk = jnp.stack([
        jnp.concatenate([new_kv[:, 0], zero], axis=2),
        jnp.concatenate([new_kv[:, 1, :, :lat], zero, new_kv[:, 1, :, lat:]], axis=2),
    ], axis=1)
    qn = [queries(layer, tiles, scale, row_slot, q_nope, q_rope, w_uk, nk) for layer in range(layers)]
    sib = [swap(q) for q, _ in qn]

    x = spread(pack(kv_cache, n_section, lat))
    x, qn = lax.optimization_barrier((x, qn))
    k0, k1 = [spread(pick(layer, lat, assign, x)) for layer in range(layers)]
    k0, sib = lax.optimization_barrier((k0, sib))
    up, down = step_y(k0, 1), step_y(k0, -1)
    up, down, k1 = lax.optimization_barrier((up, down, k1))
    near0, far0 = [k0, up, down], onward(up, down)
    up, down = step_y(k1, 1), step_y(k1, -1)
    order = (0, 1, 3, 2)

    def attended(layer, shifts, pieces, ropes):
        return attend(layer, scale, shifts, row_slot, assign, prompt_len, qn[layer][0], sib[layer], pieces, ropes)

    first = attended(0, order[:3], near0, near0)
    first, up, down = lax.optimization_barrier((first, up, down))
    p1 = [k1, up, down] + onward(up, down)
    calls = [[first, attended(0, order[3:], far0, far0)], [attended(1, order, p1, near0 + far0)]]
    out = None
    for layer in range(layers):
        partials = [x for mine, theirs in calls[layer] for x in (mine, swap(theirs))]
        out = merge(layer, layers, steps, rows, row_slot, partials + [qn[layer][1]], w_uv, out)
    return out


def solution(mesh):
    in_specs = (
        P(None, "section", "head", None),
        P(),
        P(),
        P("section"),
        P(None, None, "section", "head"),
        P(None, None, "section", "head"),
        P(None, None, "section", None),
        P(None, "head", None, None),
        P(None, "head", None, None),
    )
    out_specs = P(None, None, "section", "head")
    step = functools.partial(local, mesh.shape["section"], mesh.shape["head"])
    return jax.shard_map(step, mesh=mesh, in_specs=in_specs, out_specs=out_specs, check_vma=False)
```

time: 132 us -> 109 us (0.83)
  the two profiles are of different devices: /device:TPU:39 before, /device:TPU:1 now
where the time goes in v1:
time: 109 us; the launch traced here: 108 us
  Pallas kernels  42.5 us (39%)
  starting transfers between devices  37.1 us (34%)
  blocking collectives  12.4 us (11%)
  waiting for transfers between devices  11.7 us (11%)
  local copies, waits for them, and re-layouts  3.62 us (3%)
    pallas_call x3, Pallas kernels, attend(): pl.pallas_call(functools.partial(attend_body, layer, scale, shifts), in_s...  20.1 us
    all_to_all x2, starting transfers between devices, spread(): return lax.all_to_all(x, 'section', 0, 0, tiled=True)  13.9 us
    all_to_all x1, blocking collectives, spread(): return lax.all_to_all(x, 'section', 0, 0, tiled=True)  12.4 us
    ppermute x5, starting transfers between devices, swap(): return lax.ppermute(x, 'head', [(h, h ^ 1) for h in range(n_head)])  11.9 us
    pallas_call x2, Pallas kernels, queries(): pl.pallas_call(functools.partial(query_body, layer, steps, scale), grid=(...  11.8 us
    all_to_all x2, waiting for transfers between devices, spread(): return lax.all_to_all(x, 'section', 0, 0, tiled=True)  11.7 us
    ppermute x8, starting transfers between devices, step_y(): lax.ppermute(x, 'head', [(h, (h // 2 + k) % chips * 2 + h % 2) for h in r...  11.2 us
    pallas_call x2, Pallas kernels, merge(): pl.pallas_call(functools.partial(merge_body, layer, steps, len(partials))...  6.79 us
  transfers between devices with their start and end apart: 15, of which 2 were waited for; matrix products, arithmetic and copies ran while one was open for 0% of the time, Pallas kernels for 35%

profile of v1, /device:TPU:1, one launch (start us, length us, event | category | flops | bytes accessed | tf_op | source)
XLA Modules:
  0.0 107.7 jit_solution(11208059019145730798)
XLA Ops:
  0.0 1.3 %copy-done.5 = bf16[2,2,256,576]{2,3,1,0:T(8,128)(2,1)S(1)} copy-done((bf16[2,2,256,576]{2,3,1,0:T(8,128)(2,1)S(1)}, bf16[2,2,256,576]{2,3,1,0:T(8,128)(2,1)}, u32[]{:S(2)}) %copy-start.5) | copy-done | bytes 1179672
  1.3 1.8 %pack.1 = bf16[16,2,16,1152]{3,2,1,0:T(8,128)(2,1)} custom-call(bf16[2,2,576,256]{3,2,1,0:T(8,128)(2,1)S(1)} %bitcast.23), custom_call_target="tpu_custom_call" | custom-call | bytes 2359296 | tf_op jit(solution)/shard_map/pack/pallas_call | solution.py:37
  3.1 8.6 %all-to-all-start = ((bf16[16,2,16,1152]{3,2,1,0:T(8,128)(2,1)}), bf16[16,2,16,1152]{3,2,1,0:T(8,128)(2,1)S(1)}, u32[]{:S(2)}, u32[]{:S(2)}) async-start(bf16[16,2,16,1152]{3,2,1,0:T(8,128)(2,1)} %pack.1), calls=%async_computation | async-start | bytes 2359296 | tf_op jit(solution)/shard_map/all_to_all | solution.py:403
  11.8 0.1 maximum_bitcast_fusion
  11.9 2.2 %copy-done = bf16[2,16,128,512]{3,2,1,0:T(8,128)(2,1)S(1)} copy-done((bf16[2,16,128,512]{3,2,1,0:T(8,128)(2,1)S(1)}, bf16[2,16,128,512]{3,2,1,0:T(8,128)(2,1)}, u32[]{:S(2)}) %copy-start) | copy-done | bytes 4194328
  14.1 5.9 %queries.2 = (bf16[4,16,16,640]{3,2,1,0:T(8,128)(2,1)}, bf16[4,16,16,640]{3,2,1,0:T(8,128)(2,1)S(1)}) custom-call(s32[32]{0:T(128)S(1)} %copy-done.7, bf16[2,2,32,2048]{3,2,1,0:T(8,128)(2,1)S(1)} %copy-done.2, bf16[2,2,32,1024]{3,2,1,0:T(8,128)(2,1)S(1)} %copy-done.6, bf16[2,16,128,512]{3,2,1,0:T(8,128)(2,1)S(1)} %copy-done, ...), custom_call_target="tpu_custom_call" | custom-call | flops 134217728 | bytes 4718592 | tf_op jit(solution)/shard_map/queries/pallas_call | solution.py:177
  20.0 0.9 collective-permute-start
  21.0 5.9 %queries.3 = (bf16[4,16,16,640]{3,2,1,0:T(8,128)(2,1)}, bf16[4,16,16,640]{3,2,1,0:T(8,128)(2,1)S(1)}) custom-call(s32[32]{0:T(128)S(1)} %copy-done.7, bf16[2,2,32,2048]{3,2,1,0:T(8,128)(2,1)S(1)} %copy-done.2, bf16[2,2,32,1024]{3,2,1,0:T(8,128)(2,1)S(1)} %copy-done.6, bf16[2,16,128,512]{3,2,1,0:T(8,128)(2,1)S(1)} %copy-done, ...), custom_call_target="tpu_custom_call" | custom-call | flops 134217728 | bytes 4718592 | tf_op jit(solution)/shard_map/queries/pallas_call | solution.py:177
  26.9 0.0 collective-permute-start.1
  26.9 1.6 %all-to-all-done = bf16[16,2,16,1152]{3,2,1,0:T(8,128)(2,1)S(1)} async-done(((bf16[16,2,16,1152]{3,2,1,0:T(8,128)(2,1)}), bf16[16,2,16,1152]{3,2,1,0:T(8,128)(2,1)S(1)}, u32[]{:S(2)}, u32[]{:S(2)}) %all-to-all-start) | async-done | bytes 1179680 | tf_op jit(solution)/shard_map/all_to_all | solution.py:403
  28.5 1.5 %pick.2 = bf16[32,16,640]{2,1,0:T(8,128)(2,1)} custom-call(s32[32]{0:T(128)S(1)} %copy-done.8, bf16[32,16,1152]{2,1,0:T(8,128)(2,1)S(1)} %bitcast.20), custom_call_target="tpu_custom_call" | custom-call | bytes 2359296 | tf_op jit(solution)/shard_map/pick/pallas_call | solution.py:60
  30.0 5.4 %all-to-all-start.1 = ((bf16[16,2,16,640]{3,2,1,0:T(8,128)(2,1)}), bf16[16,2,16,640]{3,2,1,0:T(8,128)(2,1)}, u32[]{:S(2)}, u32[]{:S(2)}) async-start(bf16[16,2,16,640]{3,2,1,0:T(8,128)(2,1)} %bitcast.7), calls=%async_computation.1 | async-start | bytes 1310720 | tf_op jit(solution)/shard_map/all_to_all | solution.py:403
  35.4 10.1 %all-to-all-done.1.refs_0_.refs_5_ = bf16[16,2,16,640]{3,2,1,0:T(8,128)(2,1)} async-done(((bf16[16,2,16,640]{3,2,1,0:T(8,128)(2,1)}), bf16[16,2,16,640]{3,2,1,0:T(8,128)(2,1)}, u32[]{:S(2)}, u32[]{:S(2)}) %all-to-all-start.1) | async-done | bytes 655392 | tf_op jit(solution)/shard_map/all_to_all | solution.py:403
  45.4 1.3 %collective-permute-start.2 = (bf16[16,2,16,640]{3,2,1,0:T(8,128)(2,1)}, bf16[16,2,16,640]{3,2,1,0:T(8,128)(2,1)S(1)}, u32[]{:S(2)}, u32[]{:S(2)}) collective-permute-start(bf16[16,2,16,640]{3,2,1,0:T(8,128)(2,1)} %all-to-all-done.1.refs_0_.refs_5_), channel_id=1, source_target_pairs={{0,2},{1,3},{2,4},{3,5},{4,6},{5,7},{6,0},{7,1},{8,10},{9,11},{10,... | collective-permute-start | bytes 1966088 | tf_op jit(solution)/shard_map/ppermute | solution.py:406
  46.7 1.4 %collective-permute-start.3 = (bf16[16,2,16,640]{3,2,1,0:T(8,128)(2,1)}, bf16[16,2,16,640]{3,2,1,0:T(8,128)(2,1)S(1)}, u32[]{:S(2)}, u32[]{:S(2)}) collective-permute-start(bf16[16,2,16,640]{3,2,1,0:T(8,128)(2,1)} %all-to-all-done.1.refs_0_.refs_5_), channel_id=1, source_target_pairs={{0,6},{1,7},{2,0},{3,1},{4,2},{5,3},{6,4},{7,5},{8,14},{9,15},{10,... | collective-permute-start | bytes 1966088 | tf_op jit(solution)/shard_map/ppermute | solution.py:406
  48.2 0.6 pick.3
  48.8 0.0 copy-start.9
  48.8 12.4 %all_to_all.15.refs_0_ = bf16[16,2,16,512]{3,2,1,0:T(8,128)(2,1)S(1)} all-to-all(bf16[16,2,16,512]{3,2,1,0:T(8,128)(2,1)S(1)} %bitcast.22), channel_id=1, replica_groups=mesh['section'=16,'head'=8] {'section'}, dimensions={0} | all-to-all | bytes 1048576 | tf_op jit(solution)/shard_map/all_to_all | solution.py:403
  61.2 0.0 collective-permute-start.4
  61.2 2.7 %collective-permute-start.5 = (bf16[16,2,16,512]{3,2,1,0:T(8,128)(2,1)S(1)}, bf16[16,2,16,512]{3,2,1,0:T(8,128)(2,1)S(1)}, u32[]{:S(2)}, u32[]{:S(2)}) collective-permute-start(bf16[16,2,16,512]{3,2,1,0:T(8,128)(2,1)S(1)} %all_to_all.15.refs_0_), channel_id=1, source_target_pairs={{0,6},{1,7},{2,0},{3,1},{4,2},{5,3},{6,4},{7,5},{8,14},{9,15},{10,... | collective-permute-start | bytes 1572872 | tf_op jit(solution)/shard_map/ppermute | solution.py:406
  63.9 0.1 collective-permute-start.8
  64.0 2.9 %collective-permute-start.9 = (bf16[8,2,16,640]{3,2,1,0:T(8,128)(2,1)S(1)}, bf16[8,2,16,640]{3,2,1,0:T(8,128)(2,1)S(1)}, u32[]{:S(2)}, u32[]{:S(2)}) collective-permute-start(bf16[8,2,16,640]{3,2,1,0:T(8,128)(2,1)S(1)} %slice.27), channel_id=1, source_target_pairs={{0,6},{1,7},{2,0},{3,1},{4,2},{5,3},{6,4},{7,5},{8,14},{9,15},{10,... | collective-permute-start | bytes 983048 | tf_op jit(solution)/shard_map/ppermute | solution.py:406
  66.9 8.2 %attend.3 = (bf16[4,16,16,640]{3,2,1,0:T(8,128)(2,1)S(1)}, bf16[4,16,16,640]{3,2,1,0:T(8,128)(2,1)S(1)}) custom-call(s32[32]{0:T(128)S(1)} %copy-done.7, s32[32]{0:T(128)S(1)} %copy-done.8, s32[32]{0:T(128)S(1)} %copy-done.9, bf16[4,16,16,640]{3,2,1,0:T(8,128)(2,1)} %get-tuple-element.39.qa_ref, bf16[4,16,16,640]{3,2,1,0:T(8,128)(2,1)} %collective-permute-done.qb_ref, ...), custom_call_target="tpu_custom_call" | custom-call | flops 3623878656 | bytes 5242880 | tf_op jit(solution)/shard_map/attend/pallas_call | solution.py:316
  75.2 0.1 collective-permute-start.6
  75.3 2.7 %collective-permute-start.7 = (bf16[8,2,16,512]{3,2,1,0:T(8,128)(2,1)S(1)}, bf16[8,2,16,512]{3,2,1,0:T(8,128)(2,1)S(1)}, u32[]{:S(2)}, u32[]{:S(2)}) collective-permute-start(bf16[8,2,16,512]{3,2,1,0:T(8,128)(2,1)S(1)} %slice.25), channel_id=1, source_target_pairs={{0,6},{1,7},{2,0},{3,1},{4,2},{5,3},{6,4},{7,5},{8,14},{9,15},{10,... | collective-permute-start | bytes 786440 | tf_op jit(solution)/shard_map/ppermute | solution.py:406
  78.1 3.0 %attend.5 = (bf16[4,16,16,640]{3,2,1,0:T(8,128)(2,1)S(1)}, bf16[4,16,16,640]{3,2,1,0:T(8,128)(2,1)S(1)}) custom-call(s32[32]{0:T(128)S(1)} %copy-done.7, s32[32]{0:T(128)S(1)} %copy-done.8, s32[32]{0:T(128)S(1)} %copy-done.9, bf16[4,16,16,640]{3,2,1,0:T(8,128)(2,1)} %get-tuple-element.39.qa_ref, bf16[4,16,16,640]{3,2,1,0:T(8,128)(2,1)} %collective-permute-done.qb_ref, ...), custom_call_target="tpu_custom_call" | custom-call | flops 1207959552 | bytes 5242880 | tf_op jit(solution)/shard_map/attend/pallas_call | solution.py:316
  81.0 9.7 %collective-permute-start.12 = (bf16[4,16,16,640]{3,2,1,0:T(8,128)(2,1)S(1)}, bf16[4,16,16,640]{3,2,1,0:T(8,128)(2,1)S(1)}, u32[]{:S(2)}, u32[]{:S(2)}) collective-permute-start(bf16[4,16,16,640]{3,2,1,0:T(8,128)(2,1)S(1)} %get-tuple-element.53), channel_id=1, source_target_pairs={{0,1},{1,0},{2,3},{3,2},{4,5},{5,4},{6,7},{7,6},{8,9},{9,8},{10,11... | collective-permute-start | bytes 3932168 | tf_op jit(solution)/shard_map/ppermute | solution.py:413
  90.7 0.1 collective-permute-start.11
  90.8 8.9 %attend.4 = (bf16[4,16,16,640]{3,2,1,0:T(8,128)(2,1)S(1)}, bf16[4,16,16,640]{3,2,1,0:T(8,128)(2,1)S(1)}) custom-call(s32[32]{0:T(128)S(1)} %copy-done.7, s32[32]{0:T(128)S(1)} %copy-done.8, s32[32]{0:T(128)S(1)} %copy-done.9, bf16[4,16,16,640]{3,2,1,0:T(8,128)(2,1)} %get-tuple-element.34.qa_ref, bf16[4,16,16,640]{3,2,1,0:T(8,128)(2,1)} %collective-permute-done.1.qb_ref, ...), custom_call_target="tpu_custom_call" | custom-call | flops 4831838208 | bytes 5242880 | tf_op jit(solution)/shard_map/attend/pallas_call | solution.py:316
  99.7 1.2 %collective-permute-start.10 = (bf16[4,16,16,640]{3,2,1,0:T(8,128)(2,1)S(1)}, bf16[4,16,16,640]{3,2,1,0:T(8,128)(2,1)S(1)}, u32[]{:S(2)}, u32[]{:S(2)}) collective-permute-start(bf16[4,16,16,640]{3,2,1,0:T(8,128)(2,1)S(1)} %get-tuple-element.48), channel_id=1, source_target_pairs={{0,1},{1,0},{2,3},{3,2},{4,5},{5,4},{6,7},{7,6},{8,9},{9,8},{10,11... | collective-permute-start | bytes 3932168 | tf_op jit(solution)/shard_map/ppermute | solution.py:413
  100.9 3.8 %merge.2.refs_3_ = bf16[2,2,32,2048]{3,2,1,0:T(8,128)(2,1)} custom-call(s32[32]{0:T(128)S(1)} %copy-done.7, bf16[2,16,512,128]{3,2,1,0:T(8,128)(2,1)S(1)} %copy-done.1, bf16[4,16,16,640]{3,2,1,0:T(8,128)(2,1)S(1)} %get-tuple-element.50.refs_0_, bf16[4,16,16,640]{3,2,1,0:T(8,128)(2,1)S(1)} %collective-permute-done.11.refs_1_, ...), custom_call_target="tpu_custom_call" | custom-call | flops 134217728 | bytes 6553600 | tf_op jit(solution)/shard_map/merge/pallas_call | solution.py:378
  104.7 3.0 %merge.3 = bf16[2,2,32,2048]{3,2,1,0:T(8,128)(2,1)} custom-call(s32[32]{0:T(128)S(1)} %copy-done.7, bf16[2,16,512,128]{3,2,1,0:T(8,128)(2,1)S(1)} %copy-done.1, bf16[4,16,16,640]{3,2,1,0:T(8,128)(2,1)S(1)} %get-tuple-element.47.refs_0_, bf16[4,16,16,640]{3,2,1,0:T(8,128)(2,1)S(1)} %collective-permute-done.10.refs_1_, ...), custom_call_target="tpu_custom_call", output_to_operand_aliasing={{}: (5, {})} | custom-call | flops 134217728 | bytes 3932160 | tf_op jit(solution)/shard_map/merge/pallas_call | solution.py:378
  (42 shorter events, 0.2 us)
Async XLA Ops:
  0.0 1.3 %copy-start.5 = (bf16[2,2,256,576]{2,3,1,0:T(8,128)(2,1)S(1)}, bf16[2,2,256,576]{2,3,1,0:T(8,128)(2,1)}, u32[]{:S(2)}) copy-start(bf16[2,2,256,576]{2,3,1,0:T(8,128)(2,1)} %param.9) | copy-start | bytes 3538948
  3.1 8.6 %copy-start.10 = (bf16[2,2,32,576]{3,2,1,0:T(8,128)(2,1)S(1)}, bf16[2,2,32,576]{3,2,1,0:T(8,128)(2,1)}, u32[]{:S(2)}) copy-start(bf16[2,2,32,576]{3,2,1,0:T(8,128)(2,1)} %param.15) | copy-start | bytes 442372
  3.1 8.8 %copy-start.2 = (bf16[2,2,32,2048]{3,2,1,0:T(8,128)(2,1)S(1)}, bf16[2,2,32,2048]{3,2,1,0:T(8,128)(2,1)}, u32[]{:S(2)}) copy-start(bf16[2,2,32,2048]{3,2,1,0:T(8,128)(2,1)} %nope_ref.3) | copy-start | bytes 1572868
  3.1 8.8 %copy-start.6 = (bf16[2,2,32,1024]{3,2,1,0:T(8,128)(2,1)S(1)}, bf16[2,2,32,1024]{3,2,1,0:T(8,128)(2,1)}, u32[]{:S(2)}) copy-start(bf16[2,2,32,1024]{3,2,1,0:T(8,128)(2,1)} %rope_ref.3) | copy-start | bytes 786436
  3.1 8.8 %copy-start.7 = (s32[32]{0:T(128)S(1)}, s32[32]{0:T(128)}, u32[]{:S(2)}) copy-start(s32[32]{0:T(128)} %slot_ref.13) | copy-start | bytes 388
  3.1 25.4 %all-to-all-start = ((bf16[16,2,16,1152]{3,2,1,0:T(8,128)(2,1)}), bf16[16,2,16,1152]{3,2,1,0:T(8,128)(2,1)S(1)}, u32[]{:S(2)}, u32[]{:S(2)}) async-start(bf16[16,2,16,1152]{3,2,1,0:T(8,128)(2,1)} %pack.1), calls=%async_computation | async-start | bytes 2359296 | tf_op jit(solution)/shard_map/all_to_all | solution.py:403
  11.9 2.2 %copy-start = (bf16[2,16,128,512]{3,2,1,0:T(8,128)(2,1)S(1)}, bf16[2,16,128,512]{3,2,1,0:T(8,128)(2,1)}, u32[]{:S(2)}) copy-start(bf16[2,16,128,512]{3,2,1,0:T(8,128)(2,1)} %w_ref.5) | copy-start | bytes 12582916
  20.0 6.8 %copy-start.3 = (bf16[4,16,16,640]{3,2,1,0:T(8,128)(2,1)}, bf16[4,16,16,640]{3,2,1,0:T(8,128)(2,1)S(1)}, u32[]{:S(2)}) copy-start(bf16[4,16,16,640]{3,2,1,0:T(8,128)(2,1)S(1)} %get-tuple-element.54.refs_4_) | copy-start | bytes 3932164
  20.0 8.5 %copy-start.8 = (s32[32]{0:T(128)S(1)}, s32[32]{0:T(128)}, u32[]{:S(2)}) copy-start(s32[32]{0:T(128)} %assign_ref.9) | copy-start | bytes 388
  20.0 15.3 %collective-permute-start = (bf16[4,16,16,640]{3,2,1,0:T(8,128)(2,1)}, bf16[4,16,16,640]{3,2,1,0:T(8,128)(2,1)}, u32[]{:S(2)}, u32[]{:S(2)}) collective-permute-start(bf16[4,16,16,640]{3,2,1,0:T(8,128)(2,1)} %get-tuple-element.39.qa_ref), channel_id=1, source_target_pairs={{0,1},{1,0},{2,3},{3,2},{4,5},{5,4},{6,7},{7,6},{8,9},{9,8},{10,11... | collective-permute-start | bytes 3932168 | tf_op jit(solution)/shard_map/ppermute | solution.py:413
  26.9 8.5 %collective-permute-start.1 = (bf16[4,16,16,640]{3,2,1,0:T(8,128)(2,1)}, bf16[4,16,16,640]{3,2,1,0:T(8,128)(2,1)}, u32[]{:S(2)}, u32[]{:S(2)}) collective-permute-start(bf16[4,16,16,640]{3,2,1,0:T(8,128)(2,1)} %get-tuple-element.34.qa_ref), channel_id=1, source_target_pairs={{0,1},{1,0},{2,3},{3,2},{4,5},{5,4},{6,7},{7,6},{8,9},{9,8},{10,11... | collective-permute-start | bytes 3932168 | tf_op jit(solution)/shard_map/ppermute | solution.py:413
  30.0 15.5 %all-to-all-start.1 = ((bf16[16,2,16,640]{3,2,1,0:T(8,128)(2,1)}), bf16[16,2,16,640]{3,2,1,0:T(8,128)(2,1)}, u32[]{:S(2)}, u32[]{:S(2)}) async-start(bf16[16,2,16,640]{3,2,1,0:T(8,128)(2,1)} %bitcast.7), calls=%async_computation.1 | async-start | bytes 1310720 | tf_op jit(solution)/shard_map/all_to_all | solution.py:403
  45.4 15.7 %collective-permute-start.2 = (bf16[16,2,16,640]{3,2,1,0:T(8,128)(2,1)}, bf16[16,2,16,640]{3,2,1,0:T(8,128)(2,1)S(1)}, u32[]{:S(2)}, u32[]{:S(2)}) collective-permute-start(bf16[16,2,16,640]{3,2,1,0:T(8,128)(2,1)} %all-to-all-done.1.refs_0_.refs_5_), channel_id=1, source_target_pairs={{0,2},{1,3},{2,4},{3,5},{4,6},{5,7},{6,0},{7,1},{8,10},{9,11},{10,... | collective-permute-start | bytes 1966088 | tf_op jit(solution)/shard_map/ppermute | solution.py:406
  46.7 14.5 %collective-permute-start.3 = (bf16[16,2,16,640]{3,2,1,0:T(8,128)(2,1)}, bf16[16,2,16,640]{3,2,1,0:T(8,128)(2,1)S(1)}, u32[]{:S(2)}, u32[]{:S(2)}) collective-permute-start(bf16[16,2,16,640]{3,2,1,0:T(8,128)(2,1)} %all-to-all-done.1.refs_0_.refs_5_), channel_id=1, source_target_pairs={{0,6},{1,7},{2,0},{3,1},{4,2},{5,3},{6,4},{7,5},{8,14},{9,15},{10,... | collective-permute-start | bytes 1966088 | tf_op jit(solution)/shard_map/ppermute | solution.py:406
  48.8 18.2 %copy-start.9 = (s32[32]{0:T(128)S(1)}, s32[32]{0:T(128)}, u32[]{:S(2)}) copy-start(s32[32]{0:T(128)} %len_ref.5) | copy-start | bytes 388
  61.2 14.0 %collective-permute-start.4 = (bf16[16,2,16,512]{3,2,1,0:T(8,128)(2,1)S(1)}, bf16[16,2,16,512]{3,2,1,0:T(8,128)(2,1)S(1)}, u32[]{:S(2)}, u32[]{:S(2)}) collective-permute-start(bf16[16,2,16,512]{3,2,1,0:T(8,128)(2,1)S(1)} %all_to_all.15.refs_0_), channel_id=1, source_target_pairs={{0,2},{1,3},{2,4},{3,5},{4,6},{5,7},{6,0},{7,1},{8,10},{9,11},{10,... | collective-permute-start | bytes 1572872 | tf_op jit(solution)/shard_map/ppermute | solution.py:406
  61.2 14.0 %collective-permute-start.5 = (bf16[16,2,16,512]{3,2,1,0:T(8,128)(2,1)S(1)}, bf16[16,2,16,512]{3,2,1,0:T(8,128)(2,1)S(1)}, u32[]{:S(2)}, u32[]{:S(2)}) collective-permute-start(bf16[16,2,16,512]{3,2,1,0:T(8,128)(2,1)S(1)} %all_to_all.15.refs_0_), channel_id=1, source_target_pairs={{0,6},{1,7},{2,0},{3,1},{4,2},{5,3},{6,4},{7,5},{8,14},{9,15},{10,... | collective-permute-start | bytes 1572872 | tf_op jit(solution)/shard_map/ppermute | solution.py:406
  63.9 14.1 %collective-permute-start.8 = (bf16[8,2,16,640]{3,2,1,0:T(8,128)(2,1)S(1)}, bf16[8,2,16,640]{3,2,1,0:T(8,128)(2,1)S(1)}, u32[]{:S(2)}, u32[]{:S(2)}) collective-permute-start(bf16[8,2,16,640]{3,2,1,0:T(8,128)(2,1)S(1)} %slice.26), channel_id=1, source_target_pairs={{0,2},{1,3},{2,4},{3,5},{4,6},{5,7},{6,0},{7,1},{8,10},{9,11},{10,... | collective-permute-start | bytes 983048 | tf_op jit(solution)/shard_map/ppermute | solution.py:406
  64.0 14.0 %collective-permute-start.9 = (bf16[8,2,16,640]{3,2,1,0:T(8,128)(2,1)S(1)}, bf16[8,2,16,640]{3,2,1,0:T(8,128)(2,1)S(1)}, u32[]{:S(2)}, u32[]{:S(2)}) collective-permute-start(bf16[8,2,16,640]{3,2,1,0:T(8,128)(2,1)S(1)} %slice.27), channel_id=1, source_target_pairs={{0,6},{1,7},{2,0},{3,1},{4,2},{5,3},{6,4},{7,5},{8,14},{9,15},{10,... | collective-permute-start | bytes 983048 | tf_op jit(solution)/shard_map/ppermute | solution.py:406
  75.2 15.6 %collective-permute-start.6 = (bf16[8,2,16,512]{3,2,1,0:T(8,128)(2,1)S(1)}, bf16[8,2,16,512]{3,2,1,0:T(8,128)(2,1)S(1)}, u32[]{:S(2)}, u32[]{:S(2)}) collective-permute-start(bf16[8,2,16,512]{3,2,1,0:T(8,128)(2,1)S(1)} %slice.24), channel_id=1, source_target_pairs={{0,2},{1,3},{2,4},{3,5},{4,6},{5,7},{6,0},{7,1},{8,10},{9,11},{10,... | collective-permute-start | bytes 786440 | tf_op jit(solution)/shard_map/ppermute | solution.py:406
  75.3 15.5 %collective-permute-start.7 = (bf16[8,2,16,512]{3,2,1,0:T(8,128)(2,1)S(1)}, bf16[8,2,16,512]{3,2,1,0:T(8,128)(2,1)S(1)}, u32[]{:S(2)}, u32[]{:S(2)}) collective-permute-start(bf16[8,2,16,512]{3,2,1,0:T(8,128)(2,1)S(1)} %slice.25), channel_id=1, source_target_pairs={{0,6},{1,7},{2,0},{3,1},{4,2},{5,3},{6,4},{7,5},{8,14},{9,15},{10,... | collective-permute-start | bytes 786440 | tf_op jit(solution)/shard_map/ppermute | solution.py:406
  81.0 19.9 %copy-start.4 = (bf16[4,16,16,640]{3,2,1,0:T(8,128)(2,1)S(1)}, bf16[4,16,16,640]{3,2,1,0:T(8,128)(2,1)}, u32[]{:S(2)}) copy-start(bf16[4,16,16,640]{3,2,1,0:T(8,128)(2,1)} %copy-done.3) | copy-start | bytes 3932164
  81.0 19.8 %collective-permute-start.12 = (bf16[4,16,16,640]{3,2,1,0:T(8,128)(2,1)S(1)}, bf16[4,16,16,640]{3,2,1,0:T(8,128)(2,1)S(1)}, u32[]{:S(2)}, u32[]{:S(2)}) collective-permute-start(bf16[4,16,16,640]{3,2,1,0:T(8,128)(2,1)S(1)} %get-tuple-element.53), channel_id=1, source_target_pairs={{0,1},{1,0},{2,3},{3,2},{4,5},{5,4},{6,7},{7,6},{8,9},{9,8},{10,11... | collective-permute-start | bytes 3932168 | tf_op jit(solution)/shard_map/ppermute | solution.py:413
  90.7 10.2 %collective-permute-start.11 = (bf16[4,16,16,640]{3,2,1,0:T(8,128)(2,1)S(1)}, bf16[4,16,16,640]{3,2,1,0:T(8,128)(2,1)S(1)}, u32[]{:S(2)}, u32[]{:S(2)}) collective-permute-start(bf16[4,16,16,640]{3,2,1,0:T(8,128)(2,1)S(1)} %get-tuple-element.51), channel_id=1, source_target_pairs={{0,1},{1,0},{2,3},{3,2},{4,5},{5,4},{6,7},{7,6},{8,9},{9,8},{10,11... | collective-permute-start | bytes 3932168 | tf_op jit(solution)/shard_map/ppermute | solution.py:413
  90.8 10.1 %copy-start.1 = (bf16[2,16,512,128]{3,2,1,0:T(8,128)(2,1)S(1)}, bf16[2,16,512,128]{3,2,1,0:T(8,128)(2,1)}, u32[]{:S(2)}) copy-start(bf16[2,16,512,128]{3,2,1,0:T(8,128)(2,1)} %w_ref.7) | copy-start | bytes 12582916
  99.7 5.0 %collective-permute-start.10 = (bf16[4,16,16,640]{3,2,1,0:T(8,128)(2,1)S(1)}, bf16[4,16,16,640]{3,2,1,0:T(8,128)(2,1)S(1)}, u32[]{:S(2)}, u32[]{:S(2)}) collective-permute-start(bf16[4,16,16,640]{3,2,1,0:T(8,128)(2,1)S(1)} %get-tuple-element.48), channel_id=1, source_target_pairs={{0,1},{1,0},{2,3},{3,2},{4,5},{5,4},{6,7},{7,6},{8,9},{9,8},{10,11... | collective-permute-start | bytes 3932168 | tf_op jit(solution)/shard_map/ppermute | solution.py:413
